TPU v7x, 32 devices: a whole 2x2x4 slice. The times are simulated.
32 devices in a mesh: row: 4 (over y, x), col: 8 (over z, core).
Axes of the slice: x: 2, y: 2, z: 4, core: 2. Of those that a mesh axis runs over, the one named last changes fastest.
Arguments:
- pair_act: bfloat16 [512, 512, 128], P('row', 'col'), may hold values from -6 to 6
- out_grad: bfloat16 [512, 512, 128], P('row', 'col'), may hold values from -6 to 6
- tri_bias: bfloat16 [4, 512, 512], P(None, 'row', 'col'), may hold values from -6 to 250
- w_query: bfloat16 [128, 128], replicated, may hold values from -0.5 to 0.5
- w_key: bfloat16 [128, 128], replicated, may hold values from -0.5 to 0.5
- w_value: bfloat16 [128, 128], replicated, may hold values from -0.5 to 0.5
- w_gate: bfloat16 [128, 128], replicated, may hold values from -0.5 to 0.5
- w_out: bfloat16 [128, 128], replicated, may hold values from -0.5 to 0.5
- key_blocks: int32 [4, 3], replicated, may hold values from 0 to 3, as said below
- list_len: int32 [4], replicated, may hold values from 1 to 3, as said below
Outputs:
- d_pair: bfloat16 [512, 512, 128], P('row', 'col')
- d_bias: float32 [4, 512, 512], P(None, 'row', 'col')
- d_w_query: float32 [128, 128], replicated
- d_w_key: float32 [128, 128], replicated
- d_w_value: float32 [128, 128], replicated
- d_w_gate: float32 [128, 128], replicated
- d_w_out: float32 [128, 128], replicated
Inputs may be any that keep to these rules, and one draw needn't show every extreme that they name: `key_blocks`: entry 0 of query block b's list is b itself; its first list_len[b] entries are distinct; entries past list_len[b] are block numbers that must be ignored. `list_len`: some query block lists 3 key blocks.
All inputs are finite; a program needn't handle non-finite values.
Results may differ from a plain program's by a relative error of at most 0.015.
Values may be sent and summed in bfloat16 or wider, within the bound.
No kernel may reach another device: no remote copies, remote signals or barrier semaphores. Data moves between devices by JAX's collectives and lax.ppermute only.
A program may use at most 192 MiB of HBM per device.

v0:
```python
import functools
import math

import jax
import jax.numpy as jnp
from jax import lax
from jax.experimental import pallas as pl
from jax.experimental.pallas import tpu as pltpu
from jax.sharding import PartitionSpec as P

F32 = jnp.float32
BF16 = jnp.bfloat16
CHUNKS = 2
TOGETHER = 4
STRIP = 32
LOG2E = math.log2(math.e)
SAFE_SCORE = 30.0
VMEM_LIMIT = 56 * 1024 * 1024
SMALL_LIMIT = 16 * 1024 * 1024


def dot(a, b):
    return jnp.dot(a, b, preferred_element_type=F32)


def bias_kernel(tables_ref, lens_ref, col_pos_ref, row_pos_ref, *refs):
    *parts, out_ref = refs
    b = pl.program_id(0)
    blocks, _, heads, size, _ = out_ref.shape
    slots = tables_ref.shape[1]
    rows, _, _, tile = parts[0].shape[1:]
    per_block = size // tile
    for h in range(heads):
        for r in range(rows):
            piece = jnp.concatenate([p[0, row_pos_ref[r], h] for p in parts], axis=0)
            at = (r % per_block) * tile
            out_ref[r // per_block, 0, h, at : at + tile, :] = piece.astype(F32).T
    for h in range(heads):
        peak = jnp.max(out_ref[tables_ref[b, 0], 0, h], axis=0, keepdims=True)
        for e in range(1, slots):
            other = jnp.max(out_ref[tables_ref[b, e], 0, h], axis=0, keepdims=True)
            peak = jnp.where(e < lens_ref[b], jnp.maximum(peak, other), peak)
        for kb in range(blocks):
            out_ref[kb, 0, h] = (out_ref[kb, 0, h] - peak) * LOG2E


def shifted_bias(gathered, key_blocks, list_len, col_pos, row_pos):
    cols, rows, heads, query_tile, key_tile = gathered.shape
    blocks = key_blocks.shape[0]
    size = cols * query_tile // blocks
    per_block = size // query_tile

    def part(sub):
        return pl.BlockSpec(
            (1, rows, heads, query_tile, key_tile),
            lambda b, tables, lens, col_at, row_at: (col_at[b * per_block + sub], 0, 0, 0, 0),
        )

    return pl.pallas_call(
        bias_kernel,
        grid_spec=pltpu.PrefetchScalarGridSpec(
            num_scalar_prefetch=4,
            grid=(blocks,),
            in_specs=[part(sub) for sub in range(per_block)],
            out_specs=pl.BlockSpec((blocks, 1, heads, size, size), lambda b, *_: (0, b, 0, 0, 0)),
        ),
        out_shape=jax.ShapeDtypeStruct((blocks, blocks, heads, size, size), F32),
        compiler_params=pltpu.CompilerParams(vmem_limit_bytes=VMEM_LIMIT),
    )(key_blocks, list_len, col_pos, row_pos, *([gathered] * per_block))


def attention_kernel(dims, first, last, tables_ref, lens_ref, parity_ref, owners_ref, *refs):
    pieces, heads, head_dim, blocks, size, slots, together, inner = dims
    refs = list(refs)
    take = lambda n: [refs.pop(0) for _ in range(n)]
    inputs = take(pieces)
    bias_ref, w_all_ref, w_all_t_ref, w_out_ref = take(4)
    carried = [] if first else take(4)
    d_pair_out = take(pieces)
    if last:
        keep_out, message_out, d_w_out = take(3)
    d_bias_s, dw_qg_s, dw_kv_s, dwo_s = sums = take(4)
    (act_s, grad_s, d_pair_s, act_t_s, kv_s, kv_t_s, w_score_s, w_probs_s, d_att_s, query_s, gate_t_s, d_gated_t_s,
     score_s, d_probs_s, probs_s, ds_s, d_kv_s, att_t_s, d_query_t_s) = refs
    proj = heads * head_dim
    scale = head_dim ** (-0.5)
    tile_rows, chan = inputs[0].shape[2:]
    tokens = blocks * size
    step = pl.program_id(0)
    span = [slice(b * size, (b + 1) * size) for b in range(blocks)]
    own = [slice(h * head_dim, (h + 1) * head_dim) for h in range(heads)]
    pair = math.gcd(2, heads)
    head_lanes = [slice(h * size, (h + 1) * size) for h in range(heads)]

    @pl.when(step == 0)
    def _():
        w_score_s[...] = jnp.zeros_like(w_score_s)
        w_probs_s[...] = jnp.zeros_like(w_probs_s)
        for n, ref in enumerate(sums):
            ref[...] = jnp.zeros_like(ref) if first else carried[n][...]

    lane_head = lax.broadcasted_iota(jnp.int32, (size, proj), 1) // head_dim
    bound = jnp.float32(0.0)
    for c in range(together):
        for s in range(pieces):
            rows = aligned(owners_ref[s], tile_rows)
            act_s[c, rows, :] = inputs[s][0, c]
            grad_s[c, rows, :] = inputs[s][1, c]
        acts = act_s[c]
        grads = grad_s[c]
        acts_t = acts.T
        act_t_s[c] = acts_t
        natural = dot(acts, w_all_ref[:, : 3 * proj])
        across = dot(w_all_t_ref[...], acts_t)
        queries_t = (across[:proj] * scale).astype(BF16)
        kv_t = across[proj : 3 * proj].astype(BF16)
        gate_t = 1.0 / (1.0 + jnp.exp(-across[3 * proj :]))
        d_gated_t = dot(w_out_ref[...], grads.T)
        d_att_t = (d_gated_t * gate_t).astype(BF16)
        gate_t_s[c] = gate_t
        d_gated_t_s[c] = d_gated_t
        squares = lambda x: jnp.max(
            jnp.sum(jnp.square(x.astype(F32)).reshape(heads, head_dim, -1), axis=1)
        )
        bound = jnp.maximum(bound, squares(queries_t) * squares(kv_t[:proj]))
        queries = (natural[:, :proj] * scale).astype(BF16)
        kv = natural[:, proj:].astype(BF16)
        zero = jnp.zeros((size, proj), BF16)
        for b in range(blocks):
            kv_s[c, b] = kv[span[b]]
            kv_t_s[c, b] = kv_t[:, span[b]]
            d_att = d_att_t[:, span[b]].T
            for h in range(heads):
                w_score_s[c, b, own[h], head_lanes[h]] = queries_t[own[h], span[b]]
                w_probs_s[c, b, own[h], head_lanes[h]] = d_att_t[own[h], span[b]]
                here = lane_head == h
                query_s[c, b, h * size : (h + 1) * size, :] = jnp.where(here, queries[span[b]], zero)
                d_att_s[c, b, h * size : (h + 1) * size, :] = jnp.where(here, d_att, zero)
    d_kv_s[...] = jnp.zeros_like(d_kv_s)

    def query_block(b, live, shift):
        chosen = [tables_ref[b, e] for e in range(live)]
        strips = [
            (e, e * size + at, at) for e in range(live) for at in range(0, size, STRIP)
        ]
        rows_of = lambda x: jnp.sum(x.reshape(-1, 8, size), axis=0)
        for c in range(together):
            kv = jnp.concatenate([kv_s[c, k] for k in chosen], axis=0)
            score_s[c, : live * size, :] = dot(kv[:, :proj], w_score_s[c, b])
            d_probs_s[c, : live * size, :] = dot(kv[:, proj:], w_probs_s[c, b])
        for h in range(heads):
            lanes = head_lanes[h]
            stats = []
            for c in range(together):

                def scores(e, row, at):
                    return (
                        score_s[c, row : row + STRIP, lanes] * LOG2E
                        + bias_ref[chosen[e], b, h, at : at + STRIP, :]
                    )

                if shift:
                    peak = jnp.full((8, size), -jnp.inf, F32)
                    for strip in strips:
                        peak = jnp.maximum(
                            peak, jnp.max(scores(*strip).reshape(-1, 8, size), axis=0)
                        )
                    peak = jnp.max(peak, axis=0, keepdims=True)
                total = jnp.zeros((8, size), F32)
                mixed = jnp.zeros((8, size), F32)
                for e, row, at in strips:
                    value = scores(e, row, at)
                    weight = jnp.exp2(value - peak if shift else value)
                    total += rows_of(weight)
                    mixed += rows_of(weight * d_probs_s[c, row : row + STRIP, lanes])
                    score_s[c, row : row + STRIP, lanes] = weight
                norm = 1.0 / jnp.sum(total, axis=0, keepdims=True)
                stats.append((norm, jnp.sum(mixed, axis=0, keepdims=True) * norm))
            for e, row, at in strips:
                part = slice(row, row + STRIP)
                gathered = d_bias_s[b, e, h, at : at + STRIP, :]
                for c, (norm, delta) in enumerate(stats):
                    probs = score_s[c, part, lanes] * norm
                    d_scores = probs * (d_probs_s[c, part, lanes] - delta)
                    probs_s[c, part, lanes] = probs.astype(BF16)
                    ds_s[c, part, lanes] = d_scores.astype(BF16)
                    gathered += d_scores
                d_bias_s[b, e, h, at : at + STRIP, :] = gathered
        for c in range(together):
            kv_t = jnp.concatenate([kv_t_s[c, k] for k in chosen], axis=1)
            for h in range(0, heads, pair):
                lanes = slice(h * size, (h + pair) * size)
                both = slice(h * head_dim, (h + pair) * head_dim)
                low = slice(proj + both.start, proj + both.stop)
                att_t = dot(kv_t[low], probs_s[c, : live * size, lanes])
                d_query_t = dot(kv_t[both], ds_s[c, : live * size, lanes])
                for n in range(pair):
                    att_t_s[c, b, own[h + n], :] = att_t[own[n], head_lanes[n]]
                    d_query_t_s[c, b, own[h + n], :] = d_query_t[own[n], head_lanes[n]]
            d_values = dot(probs_s[c, : live * size, :], d_att_s[c, b])
            d_keys = dot(ds_s[c, : live * size, :], query_s[c, b])
            for e in range(live):
                part = slice(e * size, (e + 1) * size)
                d_kv_s[c, chosen[e], :, :proj] += d_keys[part]
                d_kv_s[c, chosen[e], :, proj:] += d_values[part]

    def all_blocks(shift):
        @pl.loop(0, blocks)
        def _(b):
            for live in range(1, slots + 1):

                @pl.when(lens_ref[b] == live)
                def _():
                    query_block(b, live, shift)

    small = bound <= SAFE_SCORE * SAFE_SCORE

    @pl.when(small)
    def _():
        all_blocks(False)

    @pl.when(jnp.logical_not(small))
    def _():
        all_blocks(True)

    w_qg = jnp.concatenate([w_all_ref[:, :proj], w_all_ref[:, 3 * proj :]], axis=1)
    for c in range(together):
        att_t = jnp.concatenate([att_t_s[c, b] for b in range(blocks)], axis=1)
        d_query_t = jnp.concatenate([d_query_t_s[c, b] for b in range(blocks)], axis=1)
        gate_t = gate_t_s[c]
        gated_t = (gate_t * att_t).astype(BF16)
        d_gpre_t = (d_gated_t_s[c] * att_t * gate_t * (1.0 - gate_t)).astype(BF16)
        d_qg_t = jnp.concatenate([(d_query_t * scale).astype(BF16), d_gpre_t], axis=0)
        d_kv = d_kv_s[c].reshape(tokens, 2 * proj).astype(BF16)
        d_pair = dot(d_kv, w_all_t_ref[proj : 3 * proj, :]) + dot(w_qg, d_qg_t).T
        d_pair_s[c] = d_pair
        for s in range(pieces):
            d_pair_out[s][c] = d_pair_s[c, aligned(owners_ref[s], tile_rows), :].astype(BF16)
        dw_qg_s[...] += dot(d_qg_t, act_s[c])
        dw_kv_s[...] += dot(act_t_s[c], d_kv)
        dwo_s[...] += dot(gated_t, grad_s[c])

    if not last:
        return

    @pl.when(step == pl.num_programs(0) - 1)
    def _():
        weights = [dw_qg_s[:proj, :].T, dw_kv_s[:, :proj], dw_kv_s[:, proj:], dw_qg_s[proj:, :].T]
        weights.append(dwo_s[...])
        far, each = keep_out.shape[0], keep_out.shape[1]
        tile = each // (slots * heads)
        for n, w in enumerate(weights):
            d_w_out[n * chan : (n + 1) * chan, :] = w
            message_out[far * each + n * chan : far * each + (n + 1) * chan, :] = w.astype(BF16)
        for mine in range(inner):

            @pl.when(parity_ref[0] == mine)
            def _():
                for b in range(blocks):
                    for e in range(slots):
                        for h in range(heads):
                            turned = d_bias_s[b, e, h].T.astype(BF16)
                            at = (e * heads + h) * tile
                            for sub in range(size // tile):
                                col = b * (size // tile) + sub
                                piece = turned[sub * tile : (sub + 1) * tile]
                                if col % inner == mine:
                                    keep_out[col // inner, at : at + tile, :] = piece
                                else:
                                    start = (col // inner) * each + at
                                    message_out[start : start + tile, :] = piece


def attention(
    pieces, bias, w_all, w_out, tables, lens, parity, owners, carried, last, query_tile, inner
):
    count = len(pieces)
    _, columns, tile_rows, chan = pieces[0].shape
    blocks, slots = tables.shape
    heads = bias.shape[2]
    proj = w_out.shape[0]
    tokens = tile_rows * count
    size = tokens // blocks
    together = math.gcd(TOGETHER, columns)
    dims = (count, heads, proj // heads, blocks, size, slots, together, inner)
    first = carried is None
    far = tokens // query_tile // inner

    def whole(x):
        return pl.BlockSpec(
            x.shape, lambda j, *_: (0,) * len(x.shape), pipeline_mode=pl.Buffered(1)
        )

    sums = [
        ((blocks, slots, heads, size, size), F32),
        ((2 * proj, chan), F32),
        ((chan, 2 * proj), F32),
        ((proj, chan), F32),
    ]
    if last:
        each = slots * heads * query_tile
        results = [
            ((far, each, size), BF16),
            ((far * each + 5 * chan, size), BF16),
            ((5 * chan, proj), F32),
        ]
    else:
        results = sums
    results = [((columns, tile_rows, chan), BF16)] * count + results
    results = [jax.ShapeDtypeStruct(*x) for x in results]
    scratch = [
        ((together, tokens, chan), BF16),
        ((together, tokens, chan), BF16),
        ((together, tokens, chan), F32),
        ((together, chan, tokens), BF16),
        ((together, blocks, size, 2 * proj), BF16),
        ((together, blocks, 2 * proj, size), BF16),
        ((together, blocks, proj, heads * size), BF16),
        ((together, blocks, proj, heads * size), BF16),
        ((together, blocks, heads * size, proj), BF16),
        ((together, blocks, heads * size, proj), BF16),
        ((together, proj, tokens), F32),
        ((together, proj, tokens), F32),
        ((together, slots * size, heads * size), F32),
        ((together, slots * size, heads * size), F32),
        ((together, slots * size, heads * size), BF16),
        ((together, slots * size, heads * size), BF16),
        ((together, blocks, size, 2 * proj), F32),
        ((together, blocks, proj, size), F32),
        ((together, blocks, proj, size), F32),
    ]
    scratch = [pltpu.VMEM(*x) for x in (sums if last else []) + scratch]
    fixed = [bias, w_all, w_all.T, w_out] + ([] if first else list(carried))
    scalars = [tables, lens, parity, owners]
    pairs = tokens * size * slots * heads
    outs = pl.pallas_call(
        functools.partial(attention_kernel, dims, first, last),
        grid_spec=pltpu.PrefetchScalarGridSpec(
            num_scalar_prefetch=len(scalars),
            grid=(columns // together,),
            in_specs=[
                pl.BlockSpec((2, together, tile_rows, chan), lambda j, *_: (0, j, 0, 0))
            ] * count
            + [whole(x) for x in fixed],
            out_specs=[pl.BlockSpec((together, tile_rows, chan), lambda j, *_: (j, 0, 0))] * count
            + [whole(x) for x in results[count:]],
            scratch_shapes=scratch,
        ),
        out_shape=results,
        compiler_params=pltpu.CompilerParams(vmem_limit_bytes=VMEM_LIMIT),
        cost_estimate=pl.CostEstimate(
            flops=columns * pairs * 7000,
            bytes_accessed=columns * tokens * chan * 6 + 10 * 2**20,
            transcendentals=columns * pairs,
        ),
    )(*scalars, *pieces, *fixed)
    return outs[:count], outs[count:]


def small_call(body, scalars, arrays, results, scratch=()):
    return pl.pallas_call(
        body,
        in_specs=[pl.BlockSpec(memory_space=pltpu.SMEM)] * len(scalars)
        + [pl.BlockSpec(memory_space=pltpu.VMEM)] * len(arrays),
        out_specs=[pl.BlockSpec(memory_space=pltpu.VMEM)] * len(results),
        out_shape=[jax.ShapeDtypeStruct(*x) for x in results],
        scratch_shapes=list(scratch),
        compiler_params=pltpu.CompilerParams(vmem_limit_bytes=SMALL_LIMIT),
    )(*scalars, *arrays)


def aligned(index, count):
    return pl.ds(pl.multiple_of(index * count, count), count)


def split_by_far(targets, keep, came, weights):
    far, each, lanes = keep.shape
    share = weights.shape[0] // far

    def body(targets_ref, keep_ref, came_ref, weights_ref, own_ref, *message_refs):
        for s in range(far):
            t = targets_ref[s]
            out = message_refs[s - 1] if s else own_ref
            bias = keep_ref[t].astype(F32)
            weight = weights_ref[aligned(t, share), :].astype(BF16).astype(F32)
            if came_ref is not None:
                bias += came_ref[aligned(t, each), :].astype(F32)
                rest = came_ref[far * each :, :].astype(F32)
                half = jnp.zeros_like(weight)
                for u in range(far):
                    half = jnp.where(t == u, rest[u * share : (u + 1) * share], half)
                weight += half
            out[:each, :] = bias.astype(out.dtype)
            out[each:, :] = weight.astype(out.dtype)

    results = [((each + share, lanes), F32 if s == 0 else BF16) for s in range(far)]
    return small_call(body, [targets], [keep, came, weights], results)


def split_by_row(owners, chosen, live, own, came, dims):
    rows, slots, per_block, each = dims
    lanes = own.shape[1]
    part = each // slots
    share = own.shape[0] - each

    def body(owners_ref, chosen_ref, live_ref, own_ref, *refs):
        came_refs, outs = refs[: len(came)], refs[len(came) :]
        weight = own_ref[each:, :]
        for ref in came_refs:
            weight += ref[each:, :].astype(F32)
        for s in range(rows):
            outs[s][part:, :] = weight.astype(BF16).astype(outs[s].dtype)
            outs[s][:part, :] = jnp.zeros((part, lanes), outs[s].dtype)
        for e in range(slots):
            at = slice(e * part, (e + 1) * part)
            bias = own_ref[at, :]
            for ref in came_refs:
                bias += ref[at, :].astype(F32)
            for s in range(rows):
                hit = (chosen_ref[e] == owners_ref[s] // per_block) & (e < live_ref[0])

                @pl.when(hit)
                def _():
                    outs[s][:part, :] = bias.astype(outs[s].dtype)

    results = [((part + share, lanes), F32 if s == 0 else BF16) for s in range(rows)]
    return small_call(body, [owners, chosen, live], [own, *came], results)


def add_rows(own, came, part):
    share, lanes = own.shape[0] - part, own.shape[1]

    def body(own_ref, *refs):
        came_refs, (bias_ref, weight_ref) = refs[: len(came)], refs[len(came) :]
        terms = [own_ref[...]] + [ref[...].astype(F32) for ref in came_refs]
        while len(terms) > 1:
            terms = [sum(terms[n : n + 2]) for n in range(0, len(terms), 2)]
        total = terms[0]
        bias_ref[...] = total[:part]
        weight_ref[...] = total[part:].astype(BF16)

    results = [((part, lanes), F32), ((share, lanes), BF16)]
    return small_call(body, [], [own, *came], results)


def place_weights(sources, parts, count):
    share, lanes = parts[0].shape

    def body(sources_ref, *refs):
        part_refs, out_refs, scratch = refs[: len(parts)], refs[len(parts) : -1], refs[-1]
        for s, ref in enumerate(part_refs):
            scratch[aligned(sources_ref[s], share), :] = ref[...].astype(F32)
        for n, ref in enumerate(out_refs):
            ref[...] = scratch[n * lanes : (n + 1) * lanes, :]

    rows = share * len(parts)
    results = [((rows // count, lanes), F32)] * count
    return small_call(body, [sources], parts, results, [pltpu.VMEM((rows, lanes), F32)])


class Peers:
    def __init__(self, axis, stride, count):
        self.axis, self.count = axis, count
        self.paired = count & (count - 1) == 0
        place = lax.axis_index(axis)
        self.digit = place // stride % count
        everyone = range(lax.axis_size(axis))
        self.routes = []
        for s in range(count):
            route = []
            for p in everyone:
                d = p // stride % count
                route.append((p, p + (self.step(d, s) - d) * stride))
            self.routes.append(route)

    def step(self, digit, s):
        return digit ^ s if self.paired else (digit + s) % self.count

    def target(self, s):
        return self.step(self.digit, s)

    def source(self, s):
        return self.target(s) if self.paired else (self.digit - s) % self.count

    def send(self, x, s, home=False):
        route = self.routes[s]
        if home:
            route = [(t, f) for f, t in route]
        return x if s == 0 else lax.ppermute(x, self.axis, route)

    def steps(self):
        digits = jnp.arange(self.count)
        return self.digit ^ digits if self.paired else (digits - self.digit) % self.count

    def positions(self):
        digits = jnp.arange(self.count)
        return self.digit ^ digits if self.paired else (self.digit - digits) % self.count

    def gather(self, x):
        return jnp.stack([self.send(x, s) for s in range(self.count)])

    def targets(self):
        return jnp.stack([self.target(s) for s in range(self.count)]).astype(jnp.int32)

    def sources(self):
        return jnp.stack([self.source(s) for s in range(self.count)]).astype(jnp.int32)

    def swap(self, messages):
        return [self.send(x, s + 1) for s, x in enumerate(messages)]


def on_device(
    pair_act, out_grad, tri_bias, w_query, w_key, w_value, w_gate, w_out, key_blocks, list_len
):
    row_count = lax.axis_size("row")
    col_count = lax.axis_size("col")
    tile_rows, tile_cols, chan = pair_act.shape
    heads = tri_bias.shape[0]
    query_tile = tri_bias.shape[2]
    proj = w_query.shape[1]
    blocks, slots = key_blocks.shape
    tokens = tile_rows * row_count
    size = tokens // blocks
    col_width = tile_cols // row_count
    chunks = math.gcd(CHUNKS, col_width)
    width = col_width // chunks
    inner = math.gcd(2, col_count)
    rows = Peers("row", 1, row_count)
    near = Peers("col", 1, inner)
    far = Peers("col", inner, col_count // inner)

    gathered = rows.gather(jnp.transpose(tri_bias, (0, 2, 1)))
    gathered, pair_act, out_grad = lax.optimization_barrier((gathered, pair_act, out_grad))
    both = jnp.stack([pair_act, out_grad]).reshape(2, tile_rows, row_count, chunks, width, chan)
    both = jnp.transpose(both, (2, 3, 0, 4, 1, 5))
    owners = rows.sources()
    outgoing = [
        [
            lax.dynamic_index_in_dim(both[:, c], rows.target(s), 0, keepdims=False)
            for s in range(row_count)
        ]
        for c in range(chunks)
    ]
    gathered, outgoing = lax.optimization_barrier((far.gather(gathered), outgoing))
    gathered = near.gather(gathered)
    gathered = gathered.reshape((col_count, row_count, heads, query_tile, tile_rows))
    columns = jnp.arange(col_count)
    col_pos = near.positions()[columns % inner] * far.count + far.positions()[columns // inner]
    bias = shifted_bias(
        gathered,
        key_blocks,
        list_len,
        col_pos.astype(jnp.int32),
        rows.positions().astype(jnp.int32),
    )

    parity = near.targets()[:1]
    w_all = jnp.concatenate([w_query, w_key, w_value, w_gate], axis=1)
    arrived = [[rows.send(x, s) for s, x in enumerate(part)] for part in outgoing]
    carried = None
    returned = []
    for c in range(chunks):
        d_pieces, carried = attention(
            arrived[c], bias, w_all, w_out, key_blocks, list_len, parity, owners, carried,
            c == chunks - 1, query_tile, inner,
        )
        if c < chunks - 1:
            d_pieces = [rows.send(x, s, home=True) for s, x in enumerate(d_pieces)]
        returned.append(d_pieces)
    keep, message, w_part = carried
    message, returned[:-1] = lax.optimization_barrier((message, returned[:-1]))
    far_targets, row_targets = far.targets(), rows.targets()

    each = keep.shape[1]
    own, *messages = split_by_far(far_targets, keep, near.send(message, inner - 1), w_part)
    messages, returned[-1] = lax.optimization_barrier((messages, returned[-1]))
    came = far.swap(messages)
    returned[-1] = [rows.send(x, s, home=True) for s, x in enumerate(returned[-1])]
    block = lax.axis_index("col") * query_tile // size
    chosen = lax.dynamic_index_in_dim(key_blocks, block, 0, keepdims=False)
    live = lax.dynamic_slice_in_dim(list_len, block, 1)
    per_block = size // tile_rows
    own, *messages = split_by_row(
        row_targets, chosen, live, own, came, (row_count, slots, per_block, each)
    )
    d_bias, w_part = add_rows(own, rows.swap(messages), each // slots)
    weights = place_weights(far.sources(), [far.send(w_part, s) for s in range(far.count)], 5)
    d_bias = d_bias.reshape(heads, query_tile, per_block, tile_rows)
    d_bias = lax.dynamic_index_in_dim(d_bias, rows.digit % per_block, 2, keepdims=False)


    by_step = [jnp.stack([part[s] for part in returned]) for s in range(row_count)]
    d_pair = jnp.stack(by_step)
    d_pair = jnp.take(d_pair, rows.steps(), axis=0)
    d_pair = jnp.transpose(d_pair, (3, 0, 1, 2, 4)).reshape(tile_rows, tile_cols, chan)
    return (d_pair, jnp.transpose(d_bias, (0, 2, 1)), *weights)


def solution(mesh):
    in_specs = (
        P("row", "col", None),
        P("row", "col", None),
        P(None, "row", "col"),
        P(),
        P(),
        P(),
        P(),
        P(),
        P(),
        P(),
    )
    out_specs = (P("row", "col", None), P(None, "row", "col"), P(), P(), P(), P(), P())
    return jax.shard_map(
        on_device, mesh=mesh, in_specs=in_specs, out_specs=out_specs, check_vma=False
    )
```

profile of v0, /device:TPU:0, one launch (start us, length us, event | category | flops | bytes accessed | tf_op | source)
XLA Modules:
  0.0 212.1 jit_solution(14534253903017569585)
XLA Ops:
  0.6 3.0 %collective-permute-start = (bf16[4,64,128]{2,1,0:T(8,128)(2,1)}, bf16[4,64,128]{2,1,0:T(8,128)(2,1)S(1)}, u32[]{:S(2)}, u32[]{:S(2)}) collective-permute-start(bf16[4,64,128]{2,1,0:T(8,128)(2,1)} %bitcast.93), channel_id=1, source_target_pairs={{0,8},{8,0},{16,24},{24,16},{1,9},{9,1},{17,25},{25,17},{2,10},{10... | collective-permute-start | bytes 196616 | tf_op jit(solution)/shard_map/ppermute | solution.py:489
  3.6 1.5 collective-permute-start.1
  5.2 1.1 collective-permute-done
  6.3 1.8 collective-permute-done.1
  8.1 2.4 %collective-permute-done.2 = bf16[4,64,128]{2,1,0:T(8,128)(2,1)S(1)} collective-permute-done((bf16[4,64,128]{2,1,0:T(8,128)(2,1)}, bf16[4,64,128]{2,1,0:T(8,128)(2,1)S(1)}, u32[]{:S(2)}, u32[]{:S(2)}) %collective-permute-start.2) | collective-permute-done | bytes 65568 | tf_op jit(solution)/shard_map/ppermute | solution.py:489
  10.5 0.9 pad_maximum_fusion.3
  11.4 1.6 collective-permute-start.3
  13.1 2.6 %collective-permute-start.4 = (bf16[4,4,64,128]{3,2,1,0:T(8,128)(2,1)S(1)}, bf16[4,4,64,128]{3,2,1,0:T(8,128)(2,1)S(1)}, u32[]{:S(2)}, u32[]{:S(2)}) collective-permute-start(bf16[4,4,64,128]{3,2,1,0:T(8,128)(2,1)S(1)} %pad_maximum_fusion.3), channel_id=1, source_target_pairs={{0,4},{1,5},{2,6},{3,7},{4,0},{5,1},{6,2},{7,3},{8,12},{9,13},{10,... | collective-permute-start | bytes 786440 | tf_op jit(solution)/shard_map/ppermute | solution.py:489
  15.9 3.1 %copy.26 = bf16[1,128,4,2,8,128]{5,1,4,0,3,2:T(8,128)(2,1)S(1)} copy(bf16[1,128,4,2,8,128]{5,4,3,2,1,0:T(8,128)(2,1)} %bitcast.78) | data formatting | bytes 4194304 | tf_op jit(solution)/shard_map/stack | solution.py:534
  19.0 1.4 copy.27
  21.3 1.7 dynamic-slice_bitcast_fusion
  23.0 11.1 %collective-permute-done.4 = bf16[4,4,64,128]{3,2,1,0:T(8,128)(2,1)S(1)} collective-permute-done((bf16[4,4,64,128]{3,2,1,0:T(8,128)(2,1)S(1)}, bf16[4,4,64,128]{3,2,1,0:T(8,128)(2,1)S(1)}, u32[]{:S(2)}, u32[]{:S(2)}) %collective-permute-start.4) | collective-permute-done | bytes 262176 | tf_op jit(solution)/shard_map/ppermute | solution.py:489
  36.1 0.9 collective-permute-start.10
  37.4 2.1 collective-permute-start.12
  39.5 0.8 copy.33.refs_5_
  42.7 0.9 collective-permute-start.6
  44.1 1.5 pad_maximum_fusion
  45.6 5.6 %shard_map.153.refs_4_ = f32[4,4,4,128,128]{4,3,2,1,0:T(8,128)} custom-call(s32[4,3]{1,0:T(4,128)} %tables_ref.5, s32[4]{0:T(128)} %lens_ref.5, s32[8]{0:T(128)} %multiply_add_fusion.col_pos_ref, s32[4]{0:T(128)} %iota_xor_fusion.2.row_pos_ref, bf16[8,4,4,64,128]{4,3,2,1,0:T(8,128)(2,1)} %bitcast.74, bf16[8,4,4,64,128]{4,3,2,1,0:T(8,128)(2,1)} %bitcast.75), custom_call_target="tpu_custom_call" | custom-call | tf_op jit(solution)/shard_map/pallas_call | solution.py:59
  51.2 2.1 collective-permute-start.8
  53.3 9.9 %collective-permute-done.11.refs_2_ = bf16[2,8,128,128]{3,2,1,0:T(8,128)(2,1)} collective-permute-done((bf16[2,8,128,128]{3,2,1,0:T(8,128)(2,1)}, bf16[2,8,128,128]{3,2,1,0:T(8,128)(2,1)}, u32[]{:S(2)}, u32[]{:S(2)}) %collective-permute-start.11) | collective-permute-done | bytes 524320 | tf_op jit(solution)/shard_map/ppermute | solution.py:489
  63.2 36.6 %shard_map.154 = (bf16[8,128,128]{2,1,0:T(8,128)(2,1)}, bf16[8,128,128]{2,1,0:T(8,128)(2,1)}, bf16[8,128,128]{2,1,0:T(8,128)(2,1)}, bf16[8,128,128]{2,1,0:T(8,12...) custom-call(s32[4,3]{1,0:T(4,128)} %tables_ref.5, ...), custom_call_target="tpu_custom_call" | custom-call | flops 44040192000 | bytes 13631488 | tf_op jit(solution)/shard_map/pallas_call | solution.py:336
  99.9 1.2 collective-permute-start.13
  101.6 1.8 collective-permute-start.15
  103.4 0.8 copy-done.11
  104.5 50.8 %shard_map.155 = (bf16[8,128,128]{2,1,0:T(8,128)(2,1)}, bf16[8,128,128]{2,1,0:T(8,128)(2,1)}, bf16[8,128,128]{2,1,0:T(8,128)(2,1)}, bf16[8,128,128]{2,1,0:T(8,12...) custom-call(s32[4,3]{1,0:T(4,128)} %tables_ref.5, s32[4]{0:T(128)} %lens_ref.5, ...), custom_call_target="tpu_custom_call" | custom-call | flops 44040192000 | bytes 13631488 | tf_op jit(solution)/shard_map/pallas_call | solution.py:336
  155.3 2.8 %collective-permute-start.16 = (bf16[3712,128]{1,0:T(8,128)(2,1)}, bf16[3712,128]{1,0:T(8,128)(2,1)S(1)}, u32[]{:S(2)}, u32[]{:S(2)}) collective-permute-start(bf16[3712,128]{1,0:T(8,128)(2,1)} %get-tuple-element.84), channel_id=1, source_target_pairs={{0,1},{1,0},{2,3},{3,2},{4,5},{5,4},{6,7},{7,6},{8,9},{9,8},{10,11... | collective-permute-start | bytes 2850824 | tf_op jit(solution)/shard_map/ppermute | solution.py:489
  158.2 2.3 %collective-permute-done.16.came_ref = bf16[3712,128]{1,0:T(8,128)(2,1)S(1)} collective-permute-done((bf16[3712,128]{1,0:T(8,128)(2,1)}, bf16[3712,128]{1,0:T(8,128)(2,1)S(1)}, u32[]{:S(2)}, u32[]{:S(2)}) %collective-permute-start.16) | collective-permute-done | bytes 950304 | tf_op jit(solution)/shard_map/ppermute | solution.py:489
  160.5 1.1 copy-done
  161.6 1.0 copy-done.1
  162.6 0.8 shard_map.156
  163.4 6.2 %collective-permute-start.20 = (bf16[928,128]{1,0:T(8,128)(2,1)S(1)}, bf16[928,128]{1,0:T(8,128)(2,1)S(1)}, u32[]{:S(2)}, u32[]{:S(2)}) collective-permute-start(bf16[928,128]{1,0:T(8,128)(2,1)S(1)} %get-tuple-element.101), channel_id=1, source_target_pairs={{0,2},{1,3},{2,0},{3,1},{4,6},{5,7},{6,4},{7,5},{8,10},{9,11},{10,... | collective-permute-start | bytes 712712 | tf_op jit(solution)/shard_map/ppermute | solution.py:489
  169.7 1.1 collective-permute-start.17
  170.8 2.4 %collective-permute-start.22 = (bf16[928,128]{1,0:T(8,128)(2,1)S(1)}, bf16[928,128]{1,0:T(8,128)(2,1)S(1)}, u32[]{:S(2)}, u32[]{:S(2)}) collective-permute-start(bf16[928,128]{1,0:T(8,128)(2,1)S(1)} %get-tuple-element.103), channel_id=1, source_target_pairs={{0,6},{1,7},{2,4},{3,5},{4,2},{5,3},{6,0},{7,1},{8,14},{9,15},{10,... | collective-permute-start | bytes 712712 | tf_op jit(solution)/shard_map/ppermute | solution.py:489
  175.1 2.2 %collective-permute-done.20.refs_0_ = bf16[928,128]{1,0:T(8,128)(2,1)S(1)} collective-permute-done((bf16[928,128]{1,0:T(8,128)(2,1)S(1)}, bf16[928,128]{1,0:T(8,128)(2,1)S(1)}, u32[]{:S(2)}, u32[]{:S(2)}) %collective-permute-start.20) | collective-permute-done | bytes 237600 | tf_op jit(solution)/shard_map/ppermute | solution.py:489
  177.3 2.0 collective-permute-start.19
  179.3 1.0 maximum_bitcast_fusion.1
  180.3 10.1 %collective-permute-done.21.refs_1_ = bf16[928,128]{1,0:T(8,128)(2,1)S(1)} collective-permute-done((bf16[928,128]{1,0:T(8,128)(2,1)S(1)}, bf16[928,128]{1,0:T(8,128)(2,1)S(1)}, u32[]{:S(2)}, u32[]{:S(2)}) %collective-permute-start.21) | collective-permute-done | bytes 237600 | tf_op jit(solution)/shard_map/ppermute | solution.py:489
  190.4 1.4 shard_map.157
  191.8 1.0 collective-permute-start.23
  192.8 0.8 collective-permute-start.24
  193.6 1.7 collective-permute-start.25
  195.5 1.6 pad_maximum_fusion.1
  197.1 2.5 %gather_fusion.2 = bf16[4,2,8,128,128]{4,3,2,1,0:T(8,128)(2,1)S(1)} fusion(bf16[4,2,8,128,128]{4,3,2,1,0:T(8,128)(2,1)} %pad_maximum_fusion.1, s32[1024]{0:T(1024)S(1)} %pad_clamp_fusion), kind=kCustom, calls=%fused_computation.2 | custom fusion | bytes 4194320 | tf_op jit(solution)/shard_map/jit(_take)/gather | solution.py:594
  199.7 0.7 shard_map.158
  200.4 4.4 %collective-permute-start.26 = (bf16[160,128]{1,0:T(8,128)(2,1)S(1)}, bf16[160,128]{1,0:T(8,128)(2,1)S(1)}, u32[]{:S(2)}, u32[]{:S(2)}) collective-permute-start(bf16[160,128]{1,0:T(8,128)(2,1)S(1)} %get-tuple-element.109.refs_0_), channel_id=1, source_target_pairs={{0,2},{1,3},{2,0},{3,1},{4,6},{5,7},{6,4},{7,5},{8,10},{9,11},{10,... | collective-permute-start | bytes 122888 | tf_op jit(solution)/shard_map/ppermute | solution.py:489
  204.8 2.4 %collective-permute-start.28 = (bf16[160,128]{1,0:T(8,128)(2,1)S(1)}, bf16[160,128]{1,0:T(8,128)(2,1)S(1)}, u32[]{:S(2)}, u32[]{:S(2)}) collective-permute-start(bf16[160,128]{1,0:T(8,128)(2,1)S(1)} %get-tuple-element.109.refs_0_), channel_id=1, source_target_pairs={{0,6},{1,7},{2,4},{3,5},{4,2},{5,3},{6,0},{7,1},{8,14},{9,15},{10,... | collective-permute-start | bytes 122888 | tf_op jit(solution)/shard_map/ppermute | solution.py:489
  207.4 2.7 %copy.34 = bf16[128,64,128]{2,1,0:T(8,128)(2,1)} copy(bf16[128,64,128]{2,0,1:T(8,128)(2,1)S(1)} %bitcast.76) | data formatting | bytes 4194304
  210.6 1.3 shard_map.159
  (81 shorter events, 10.1 us)
Async XLA Ops:
  0.6 5.7 %collective-permute-start = (bf16[4,64,128]{2,1,0:T(8,128)(2,1)}, bf16[4,64,128]{2,1,0:T(8,128)(2,1)S(1)}, u32[]{:S(2)}, u32[]{:S(2)}) collective-permute-start(bf16[4,64,128]{2,1,0:T(8,128)(2,1)} %bitcast.93), channel_id=1, source_target_pairs={{0,8},{8,0},{16,24},{24,16},{1,9},{9,1},{17,25},{25,17},{2,10},{10... | collective-permute-start | bytes 196616 | tf_op jit(solution)/shard_map/ppermute | solution.py:489
  3.6 4.5 %collective-permute-start.1 = (bf16[4,64,128]{2,1,0:T(8,128)(2,1)}, bf16[4,64,128]{2,1,0:T(8,128)(2,1)S(1)}, u32[]{:S(2)}, u32[]{:S(2)}) collective-permute-start(bf16[4,64,128]{2,1,0:T(8,128)(2,1)} %bitcast.94), channel_id=1, source_target_pairs={{0,16},{8,24},{16,0},{24,8},{1,17},{9,25},{17,1},{25,9},{2,18},{10... | collective-permute-start | bytes 196616 | tf_op jit(solution)/shard_map/ppermute | solution.py:489
  5.2 5.4 %collective-permute-start.2 = (bf16[4,64,128]{2,1,0:T(8,128)(2,1)}, bf16[4,64,128]{2,1,0:T(8,128)(2,1)S(1)}, u32[]{:S(2)}, u32[]{:S(2)}) collective-permute-start(bf16[4,64,128]{2,1,0:T(8,128)(2,1)} %bitcast.95), channel_id=1, source_target_pairs={{0,24},{8,16},{16,8},{24,0},{1,25},{9,17},{17,9},{25,1},{2,26},{10... | collective-permute-start | bytes 196616 | tf_op jit(solution)/shard_map/ppermute | solution.py:489
  11.4 11.6 %collective-permute-start.3 = (bf16[4,4,64,128]{3,2,1,0:T(8,128)(2,1)S(1)}, bf16[4,4,64,128]{3,2,1,0:T(8,128)(2,1)S(1)}, u32[]{:S(2)}, u32[]{:S(2)}) collective-permute-start(bf16[4,4,64,128]{3,2,1,0:T(8,128)(2,1)S(1)} %pad_maximum_fusion.3), channel_id=1, source_target_pairs={{0,2},{1,3},{2,0},{3,1},{4,6},{5,7},{6,4},{7,5},{8,10},{9,11},{10,... | collective-permute-start | bytes 786440 | tf_op jit(solution)/shard_map/ppermute | solution.py:489
  13.1 21.0 %collective-permute-start.4 = (bf16[4,4,64,128]{3,2,1,0:T(8,128)(2,1)S(1)}, bf16[4,4,64,128]{3,2,1,0:T(8,128)(2,1)S(1)}, u32[]{:S(2)}, u32[]{:S(2)}) collective-permute-start(bf16[4,4,64,128]{3,2,1,0:T(8,128)(2,1)S(1)} %pad_maximum_fusion.3), channel_id=1, source_target_pairs={{0,4},{1,5},{2,6},{3,7},{4,0},{5,1},{6,2},{7,3},{8,12},{9,13},{10,... | collective-permute-start | bytes 786440 | tf_op jit(solution)/shard_map/ppermute | solution.py:489
  15.6 18.5 %collective-permute-start.5 = (bf16[4,4,64,128]{3,2,1,0:T(8,128)(2,1)S(1)}, bf16[4,4,64,128]{3,2,1,0:T(8,128)(2,1)S(1)}, u32[]{:S(2)}, u32[]{:S(2)}) collective-permute-start(bf16[4,4,64,128]{3,2,1,0:T(8,128)(2,1)S(1)} %pad_maximum_fusion.3), channel_id=1, source_target_pairs={{0,6},{1,7},{2,4},{3,5},{4,2},{5,3},{6,0},{7,1},{8,14},{9,15},{10,... | collective-permute-start | bytes 786440 | tf_op jit(solution)/shard_map/ppermute | solution.py:489
  15.9 3.1 %copy-start.3 = (bf16[128,64,128]{2,1,0:T(8,128)(2,1)S(1)}, bf16[128,64,128]{2,1,0:T(8,128)(2,1)}, u32[]{:S(2)}) copy-start(bf16[128,64,128]{2,1,0:T(8,128)(2,1)} %param.11) | copy-start | bytes 6291460
  23.0 11.8 %copy-start.5 = (bf16[128,128]{1,0:T(8,128)(2,1)S(1)}, bf16[128,128]{1,0:T(8,128)(2,1)}, u32[]{:S(2)}) copy-start(bf16[128,128]{1,0:T(8,128)(2,1)} %param.13) | copy-start | bytes 98308
  23.0 11.9 %copy-start.6 = (bf16[128,128]{1,0:T(8,128)(2,1)S(1)}, bf16[128,128]{1,0:T(8,128)(2,1)}, u32[]{:S(2)}) copy-start(bf16[128,128]{1,0:T(8,128)(2,1)} %param.14) | copy-start | bytes 98308
  23.0 12.0 %copy-start.7 = (bf16[128,128]{1,0:T(8,128)(2,1)S(1)}, bf16[128,128]{1,0:T(8,128)(2,1)}, u32[]{:S(2)}) copy-start(bf16[128,128]{1,0:T(8,128)(2,1)} %param.15) | copy-start | bytes 98308
  23.0 12.2 %copy-start.8 = (bf16[128,128]{1,0:T(8,128)(2,1)S(1)}, bf16[128,128]{1,0:T(8,128)(2,1)}, u32[]{:S(2)}) copy-start(bf16[128,128]{1,0:T(8,128)(2,1)} %param.16) | copy-start | bytes 98308
  34.2 9.4 %collective-permute-start.9 = (bf16[4,4,4,64,128]{4,3,2,1,0:T(8,128)(2,1)S(1)}, bf16[4,4,4,64,128]{4,3,2,1,0:T(8,128)(2,1)S(1)}, u32[]{:S(2)}, u32[]{:S(2)}) collective-permute-start(bf16[4,4,4,64,128]{4,3,2,1,0:T(8,128)(2,1)S(1)} %pad_maximum_fusion.2), channel_id=1, source_target_pairs={{0,1},{1,0},{2,3},{3,2},{4,5},{5,4},{6,7},{7,6},{8,9},{9,8},{10,11... | collective-permute-start | bytes 3145736 | tf_op jit(solution)/shard_map/ppermute | solution.py:489
  36.1 15.1 %collective-permute-start.10 = (bf16[2,8,128,128]{3,2,1,0:T(8,128)(2,1)}, bf16[2,8,128,128]{3,2,1,0:T(8,128)(2,1)}, u32[]{:S(2)}, u32[]{:S(2)}) collective-permute-start(bf16[2,8,128,128]{3,2,1,0:T(8,128)(2,1)} %get-tuple-element.70), channel_id=1, source_target_pairs={{0,8},{8,0},{16,24},{24,16},{1,9},{9,1},{17,25},{25,17},{2,10},{10... | collective-permute-start | bytes 1572872 | tf_op jit(solution)/shard_map/ppermute | solution.py:489
  36.9 26.3 %collective-permute-start.11 = (bf16[2,8,128,128]{3,2,1,0:T(8,128)(2,1)}, bf16[2,8,128,128]{3,2,1,0:T(8,128)(2,1)}, u32[]{:S(2)}, u32[]{:S(2)}) collective-permute-start(bf16[2,8,128,128]{3,2,1,0:T(8,128)(2,1)} %get-tuple-element.71), channel_id=1, source_target_pairs={{0,16},{8,24},{16,0},{24,8},{1,17},{9,25},{17,1},{25,9},{2,18},{10... | collective-permute-start | bytes 1572872 | tf_op jit(solution)/shard_map/ppermute | solution.py:489
  37.4 25.8 %collective-permute-start.12 = (bf16[2,8,128,128]{3,2,1,0:T(8,128)(2,1)}, bf16[2,8,128,128]{3,2,1,0:T(8,128)(2,1)}, u32[]{:S(2)}, u32[]{:S(2)}) collective-permute-start(bf16[2,8,128,128]{3,2,1,0:T(8,128)(2,1)} %get-tuple-element.72), channel_id=1, source_target_pairs={{0,24},{8,16},{16,8},{24,0},{1,25},{9,17},{17,9},{25,1},{2,26},{10... | collective-permute-start | bytes 1572872 | tf_op jit(solution)/shard_map/ppermute | solution.py:489
  42.7 58.9 %collective-permute-start.6 = (bf16[2,8,128,128]{3,2,1,0:T(8,128)(2,1)}, bf16[2,8,128,128]{3,2,1,0:T(8,128)(2,1)S(1)}, u32[]{:S(2)}, u32[]{:S(2)}) collective-permute-start(bf16[2,8,128,128]{3,2,1,0:T(8,128)(2,1)} %get-tuple-element.65), channel_id=1, source_target_pairs={{0,8},{8,0},{16,24},{24,16},{1,9},{9,1},{17,25},{25,17},{2,10},{10... | collective-permute-start | bytes 1572872 | tf_op jit(solution)/shard_map/ppermute | solution.py:489
  43.6 59.8 %collective-permute-start.7 = (bf16[2,8,128,128]{3,2,1,0:T(8,128)(2,1)S(1)}, bf16[2,8,128,128]{3,2,1,0:T(8,128)(2,1)S(1)}, u32[]{:S(2)}, u32[]{:S(2)}) collective-permute-start(bf16[2,8,128,128]{3,2,1,0:T(8,128)(2,1)S(1)} %get-tuple-element.66), channel_id=1, source_target_pairs={{0,16},{8,24},{16,0},{24,8},{1,17},{9,25},{17,1},{25,9},{2,18},{10... | collective-permute-start | bytes 1572872 | tf_op jit(solution)/shard_map/ppermute | solution.py:489
  51.2 52.2 %collective-permute-start.8 = (bf16[2,8,128,128]{3,2,1,0:T(8,128)(2,1)S(1)}, bf16[2,8,128,128]{3,2,1,0:T(8,128)(2,1)S(1)}, u32[]{:S(2)}, u32[]{:S(2)}) collective-permute-start(bf16[2,8,128,128]{3,2,1,0:T(8,128)(2,1)S(1)} %get-tuple-element.67), channel_id=1, source_target_pairs={{0,24},{8,16},{16,8},{24,0},{1,25},{9,17},{17,9},{25,1},{2,26},{10... | collective-permute-start | bytes 1572872 | tf_op jit(solution)/shard_map/ppermute | solution.py:489
  99.9 55.5 %collective-permute-start.13 = (bf16[8,128,128]{2,1,0:T(8,128)(2,1)}, bf16[8,128,128]{2,1,0:T(8,128)(2,1)S(1)}, u32[]{:S(2)}, u32[]{:S(2)}) collective-permute-start(bf16[8,128,128]{2,1,0:T(8,128)(2,1)} %get-tuple-element.79), channel_id=1, source_target_pairs={{8,0},{0,8},{24,16},{16,24},{9,1},{1,9},{25,17},{17,25},{10,2},{2,... | collective-permute-start | bytes 786440 | tf_op jit(solution)/shard_map/ppermute | solution.py:489
  101.1 54.2 %collective-permute-start.14 = (bf16[8,128,128]{2,1,0:T(8,128)(2,1)}, bf16[8,128,128]{2,1,0:T(8,128)(2,1)S(1)}, u32[]{:S(2)}, u32[]{:S(2)}) collective-permute-start(bf16[8,128,128]{2,1,0:T(8,128)(2,1)} %get-tuple-element.80), channel_id=1, source_target_pairs={{16,0},{24,8},{0,16},{8,24},{17,1},{25,9},{1,17},{9,25},{18,2},{26... | collective-permute-start | bytes 786440 | tf_op jit(solution)/shard_map/ppermute | solution.py:489
  101.6 1.8 copy-start.10
  101.6 53.7 %collective-permute-start.15 = (bf16[8,128,128]{2,1,0:T(8,128)(2,1)}, bf16[8,128,128]{2,1,0:T(8,128)(2,1)S(1)}, u32[]{:S(2)}, u32[]{:S(2)}) collective-permute-start(bf16[8,128,128]{2,1,0:T(8,128)(2,1)} %get-tuple-element.81), channel_id=1, source_target_pairs={{24,0},{16,8},{8,16},{0,24},{25,1},{17,9},{9,17},{1,25},{26,2},{18... | collective-permute-start | bytes 786440 | tf_op jit(solution)/shard_map/ppermute | solution.py:489
  103.4 0.8 copy-start.11
  103.4 1.0 copy-start.12
  104.5 74.8 %copy-start.4 = (bf16[8,128,128]{2,1,0:T(8,128)(2,1)S(1)}, bf16[8,128,128]{2,1,0:T(8,128)(2,1)}, u32[]{:S(2)}) copy-start(bf16[8,128,128]{2,1,0:T(8,128)(2,1)} %get-tuple-element.82) | copy-start | bytes 786436
  155.3 19.2 %copy-start.9 = (s32[4]{0:T(128)S(1)}, s32[4]{0:T(128)}, u32[]{:S(2)}) copy-start(s32[4]{0:T(128)} %lens_ref.5) | copy-start | bytes 52
  155.3 35.1 %copy-start.2 = (s32[4]{0:T(128)S(1)}, s32[4]{0:T(128)}, u32[]{:S(2)}) copy-start(s32[4]{0:T(128)} %pad_add_fusion.owners_ref) | copy-start | bytes 52
  155.3 5.2 %collective-permute-start.16 = (bf16[3712,128]{1,0:T(8,128)(2,1)}, bf16[3712,128]{1,0:T(8,128)(2,1)S(1)}, u32[]{:S(2)}, u32[]{:S(2)}) collective-permute-start(bf16[3712,128]{1,0:T(8,128)(2,1)} %get-tuple-element.84), channel_id=1, source_target_pairs={{0,1},{1,0},{2,3},{3,2},{4,5},{5,4},{6,7},{7,6},{8,9},{9,8},{10,11... | collective-permute-start | bytes 2850824 | tf_op jit(solution)/shard_map/ppermute | solution.py:489
  160.5 1.1 copy-start
  161.6 1.0 copy-start.1
  163.4 13.8 %collective-permute-start.20 = (bf16[928,128]{1,0:T(8,128)(2,1)S(1)}, bf16[928,128]{1,0:T(8,128)(2,1)S(1)}, u32[]{:S(2)}, u32[]{:S(2)}) collective-permute-start(bf16[928,128]{1,0:T(8,128)(2,1)S(1)} %get-tuple-element.101), channel_id=1, source_target_pairs={{0,2},{1,3},{2,0},{3,1},{4,6},{5,7},{6,4},{7,5},{8,10},{9,11},{10,... | collective-permute-start | bytes 712712 | tf_op jit(solution)/shard_map/ppermute | solution.py:489
  169.7 23.9 %collective-permute-start.17 = (bf16[8,128,128]{2,1,0:T(8,128)(2,1)}, bf16[8,128,128]{2,1,0:T(8,128)(2,1)S(1)}, u32[]{:S(2)}, u32[]{:S(2)}) collective-permute-start(bf16[8,128,128]{2,1,0:T(8,128)(2,1)} %get-tuple-element.95), channel_id=1, source_target_pairs={{8,0},{0,8},{24,16},{16,24},{9,1},{1,9},{25,17},{17,25},{10,2},{2,... | collective-permute-start | bytes 786440 | tf_op jit(solution)/shard_map/ppermute | solution.py:489
  170.8 19.6 %collective-permute-start.21 = (bf16[928,128]{1,0:T(8,128)(2,1)S(1)}, bf16[928,128]{1,0:T(8,128)(2,1)S(1)}, u32[]{:S(2)}, u32[]{:S(2)}) collective-permute-start(bf16[928,128]{1,0:T(8,128)(2,1)S(1)} %get-tuple-element.102), channel_id=1, source_target_pairs={{0,4},{1,5},{2,6},{3,7},{4,0},{5,1},{6,2},{7,3},{8,12},{9,13},{10,... | collective-permute-start | bytes 712712 | tf_op jit(solution)/shard_map/ppermute | solution.py:489
  170.8 19.6 %collective-permute-start.22 = (bf16[928,128]{1,0:T(8,128)(2,1)S(1)}, bf16[928,128]{1,0:T(8,128)(2,1)S(1)}, u32[]{:S(2)}, u32[]{:S(2)}) collective-permute-start(bf16[928,128]{1,0:T(8,128)(2,1)S(1)} %get-tuple-element.103), channel_id=1, source_target_pairs={{0,6},{1,7},{2,4},{3,5},{4,2},{5,3},{6,0},{7,1},{8,14},{9,15},{10,... | collective-permute-start | bytes 712712 | tf_op jit(solution)/shard_map/ppermute | solution.py:489
  173.2 22.1 %collective-permute-start.18 = (bf16[8,128,128]{2,1,0:T(8,128)(2,1)}, bf16[8,128,128]{2,1,0:T(8,128)(2,1)S(1)}, u32[]{:S(2)}, u32[]{:S(2)}) collective-permute-start(bf16[8,128,128]{2,1,0:T(8,128)(2,1)} %get-tuple-element.97), channel_id=1, source_target_pairs={{16,0},{24,8},{0,16},{8,24},{17,1},{25,9},{1,17},{9,25},{18,2},{26... | collective-permute-start | bytes 786440 | tf_op jit(solution)/shard_map/ppermute | solution.py:489
  177.3 18.2 %collective-permute-start.19 = (bf16[8,128,128]{2,1,0:T(8,128)(2,1)}, bf16[8,128,128]{2,1,0:T(8,128)(2,1)S(1)}, u32[]{:S(2)}, u32[]{:S(2)}) collective-permute-start(bf16[8,128,128]{2,1,0:T(8,128)(2,1)} %get-tuple-element.99), channel_id=1, source_target_pairs={{24,0},{16,8},{8,16},{0,24},{25,1},{17,9},{9,17},{1,25},{26,2},{18... | collective-permute-start | bytes 786440 | tf_op jit(solution)/shard_map/ppermute | solution.py:489
  191.8 7.9 %collective-permute-start.23 = (bf16[416,128]{1,0:T(8,128)(2,1)S(1)}, bf16[416,128]{1,0:T(8,128)(2,1)S(1)}, u32[]{:S(2)}, u32[]{:S(2)}) collective-permute-start(bf16[416,128]{1,0:T(8,128)(2,1)S(1)} %get-tuple-element.105), channel_id=1, source_target_pairs={{0,8},{8,0},{16,24},{24,16},{1,9},{9,1},{17,25},{25,17},{2,10},{10... | collective-permute-start | bytes 319496 | tf_op jit(solution)/shard_map/ppermute | solution.py:489
  192.8 6.9 %collective-permute-start.24 = (bf16[416,128]{1,0:T(8,128)(2,1)S(1)}, bf16[416,128]{1,0:T(8,128)(2,1)S(1)}, u32[]{:S(2)}, u32[]{:S(2)}) collective-permute-start(bf16[416,128]{1,0:T(8,128)(2,1)S(1)} %get-tuple-element.106), channel_id=1, source_target_pairs={{0,16},{8,24},{16,0},{24,8},{1,17},{9,25},{17,1},{25,9},{2,18},{10... | collective-permute-start | bytes 319496 | tf_op jit(solution)/shard_map/ppermute | solution.py:489
  193.6 6.1 %collective-permute-start.25 = (bf16[416,128]{1,0:T(8,128)(2,1)S(1)}, bf16[416,128]{1,0:T(8,128)(2,1)S(1)}, u32[]{:S(2)}, u32[]{:S(2)}) collective-permute-start(bf16[416,128]{1,0:T(8,128)(2,1)S(1)} %get-tuple-element.107), channel_id=1, source_target_pairs={{0,24},{8,16},{16,8},{24,0},{1,25},{9,17},{17,9},{25,1},{2,26},{10... | collective-permute-start | bytes 319496 | tf_op jit(solution)/shard_map/ppermute | solution.py:489
  200.4 9.7 %collective-permute-start.26 = (bf16[160,128]{1,0:T(8,128)(2,1)S(1)}, bf16[160,128]{1,0:T(8,128)(2,1)S(1)}, u32[]{:S(2)}, u32[]{:S(2)}) collective-permute-start(bf16[160,128]{1,0:T(8,128)(2,1)S(1)} %get-tuple-element.109.refs_0_), channel_id=1, source_target_pairs={{0,2},{1,3},{2,0},{3,1},{4,6},{5,7},{6,4},{7,5},{8,10},{9,11},{10,... | collective-permute-start | bytes 122888 | tf_op jit(solution)/shard_map/ppermute | solution.py:489
  204.8 5.3 %collective-permute-start.27 = (bf16[160,128]{1,0:T(8,128)(2,1)S(1)}, bf16[160,128]{1,0:T(8,128)(2,1)S(1)}, u32[]{:S(2)}, u32[]{:S(2)}) collective-permute-start(bf16[160,128]{1,0:T(8,128)(2,1)S(1)} %get-tuple-element.109.refs_0_), channel_id=1, source_target_pairs={{0,4},{1,5},{2,6},{3,7},{4,0},{5,1},{6,2},{7,3},{8,12},{9,13},{10,... | collective-permute-start | bytes 122888 | tf_op jit(solution)/shard_map/ppermute | solution.py:489
  204.8 5.8 %collective-permute-start.28 = (bf16[160,128]{1,0:T(8,128)(2,1)S(1)}, bf16[160,128]{1,0:T(8,128)(2,1)S(1)}, u32[]{:S(2)}, u32[]{:S(2)}) collective-permute-start(bf16[160,128]{1,0:T(8,128)(2,1)S(1)} %get-tuple-element.109.refs_0_), channel_id=1, source_target_pairs={{0,6},{1,7},{2,4},{3,5},{4,2},{5,3},{6,0},{7,1},{8,14},{9,15},{10,... | collective-permute-start | bytes 122888 | tf_op jit(solution)/shard_map/ppermute | solution.py:489
where the time goes:
time: 215 us; the launch traced here: 212 us
  Pallas kernels  97.2 us (45%)
  starting transfers between devices  45.1 us (21%)
  waiting for transfers between devices  41.5 us (19%)
  local copies, waits for them, and re-layouts  18.9 us (9%)
  other arithmetic  8.3 us (4%)
    pallas_call x2, Pallas kernels, attention(): pl.pallas_call(functools.partial(attention_kernel, dims, first, last), gr...  87.4 us
    ppermute x29, starting transfers between devices, send(): return x if s == 0 else lax.ppermute(x, self.axis, route)  45.1 us
    ppermute x29, waiting for transfers between devices, send(): return x if s == 0 else lax.ppermute(x, self.axis, route)  41.5 us
    unnamed x31, local copies, waits for them, and re-layouts  6.28 us
    pallas_call x1, Pallas kernels, shifted_bias(): pl.pallas_call(bias_kernel, grid_spec=pltpu.PrefetchScalarGridSpec(num_sc...  5.57 us
    another operation x2, local copies, waits for them, and re-layouts, on_device(): jnp.stack([pair_act, out_grad])  4.45 us
  transfers between devices with their start and end apart: 29, of which 9 were waited for; matrix products, arithmetic and copies ran while one was open for 11% of the time, Pallas kernels for 45%

commit v1 on v0

--- a/solution.py
+++ b/solution.py
@@ -11,7 +11,7 @@
 F32 = jnp.float32
 BF16 = jnp.bfloat16
 CHUNKS = 2
-TOGETHER = 4
+TOGETHER = 2
 STRIP = 32
 LOG2E = math.log2(math.e)
 SAFE_SCORE = 30.0
@@ -488,10 +488,6 @@
             route = [(t, f) for f, t in route]
         return x if s == 0 else lax.ppermute(x, self.axis, route)
 
-    def steps(self):
-        digits = jnp.arange(self.count)
-        return self.digit ^ digits if self.paired else (digits - self.digit) % self.count
-
     def positions(self):
         digits = jnp.arange(self.count)
         return self.digit ^ digits if self.paired else (self.digit - digits) % self.count
@@ -530,7 +526,6 @@
     far = Peers("col", inner, col_count // inner)
 
     gathered = rows.gather(jnp.transpose(tri_bias, (0, 2, 1)))
-    gathered, pair_act, out_grad = lax.optimization_barrier((gathered, pair_act, out_grad))
     both = jnp.stack([pair_act, out_grad]).reshape(2, tile_rows, row_count, chunks, width, chan)
     both = jnp.transpose(both, (2, 3, 0, 4, 1, 5))
     owners = rows.sources()
@@ -541,7 +536,11 @@
         ]
         for c in range(chunks)
     ]
-    gathered, outgoing = lax.optimization_barrier((far.gather(gathered), outgoing))
+    gathered, outgoing = lax.optimization_barrier((gathered, outgoing))
+    arrived = [[rows.send(x, s) for s, x in enumerate(outgoing[0])]]
+    gathered, arrived[0], outgoing[1:] = lax.optimization_barrier(
+        (far.gather(gathered), arrived[0], outgoing[1:])
+    )
     gathered = near.gather(gathered)
     gathered = gathered.reshape((col_count, row_count, heads, query_tile, tile_rows))
     columns = jnp.arange(col_count)
@@ -556,7 +555,7 @@
 
     parity = near.targets()[:1]
     w_all = jnp.concatenate([w_query, w_key, w_value, w_gate], axis=1)
-    arrived = [[rows.send(x, s) for s, x in enumerate(part)] for part in outgoing]
+    arrived += [[rows.send(x, s) for s, x in enumerate(part)] for part in outgoing[1:]]
     carried = None
     returned = []
     for c in range(chunks):
@@ -589,10 +588,11 @@
     d_bias = lax.dynamic_index_in_dim(d_bias, rows.digit % per_block, 2, keepdims=False)
 
 
-    by_step = [jnp.stack([part[s] for part in returned]) for s in range(row_count)]
-    d_pair = jnp.stack(by_step)
-    d_pair = jnp.take(d_pair, rows.steps(), axis=0)
-    d_pair = jnp.transpose(d_pair, (3, 0, 1, 2, 4)).reshape(tile_rows, tile_cols, chan)
+    d_pair = jnp.zeros((tile_rows, tile_cols, chan), BF16)
+    for c, part in enumerate(returned):
+        for s, x in enumerate(part):
+            at = rows.target(s) * col_width + c * width
+            d_pair = lax.dynamic_update_slice(d_pair, jnp.transpose(x, (1, 0, 2)), (0, at, 0))
     return (d_pair, jnp.transpose(d_bias, (0, 2, 1)), *weights)
 
 

time: 215 us -> 194 us (0.902); the launches traced: 212 us -> 197 us
  waiting for transfers between devices: 41.5 us -> 36.3 us
  other arithmetic: 8.3 us -> 4.57 us
  Pallas kernels: 97.2 us -> 93.5 us
  local copies, waits for them, and re-layouts: 18.9 us -> 16.7 us
    ppermute x29, waiting for transfers between devices: 41.5 us -> 36.3 us  [send(): return x if s == 0 else lax.ppermute(x, self.axis, route)]
    unnamed x31 -> x42, local copies, waits for them, and re-layouts: 6.28 us -> 1.5 us
    pallas_call x2, Pallas kernels: 87.4 us -> 83.6 us  [attention(): pl.pallas_call(functools.partial(attention_kernel, dims, first, last), gr...]
    another operation x5 -> x0, other arithmetic: 2.73 us -> none  [on_device(): d_pair = jnp.stack(by_step)]
    gather x1 -> x0, local copies, waits for them, and re-layouts: 2.54 us -> none  [on_device(): d_pair = jnp.take(d_pair, rows.steps(), axis=0)]
  transfers between devices with their start and end apart: 29 -> 29, of which waited for: 9 -> 10; matrix products, arithmetic and copies ran while one was open for 11% -> 10% of each run, Pallas kernels for 45% -> 46%
where the time goes in v1:
time: 194 us; the launch traced here: 197 us
  Pallas kernels  93.5 us (48%)
  starting transfers between devices  44.6 us (23%)
  waiting for transfers between devices  36.3 us (19%)
  local copies, waits for them, and re-layouts  16.7 us (9%)
  other arithmetic  4.57 us (2%)
    pallas_call x2, Pallas kernels, attention(): pl.pallas_call(functools.partial(attention_kernel, dims, first, last), gr...  83.6 us
    ppermute x29, starting transfers between devices, send(): return x if s == 0 else lax.ppermute(x, self.axis, route)  44.6 us
    ppermute x29, waiting for transfers between devices, send(): return x if s == 0 else lax.ppermute(x, self.axis, route)  36.3 us
    pallas_call x1, Pallas kernels, shifted_bias(): pl.pallas_call(bias_kernel, grid_spec=pltpu.PrefetchScalarGridSpec(num_sc...  5.71 us
    another operation x2, local copies, waits for them, and re-layouts, on_device(): jnp.stack([pair_act, out_grad])  4.45 us
    pallas_call x4, Pallas kernels, small_call(): pl.pallas_call(body, in_specs=[pl.BlockSpec(memory_space=pltpu.SMEM)] * l...  4.22 us
  transfers between devices with their start and end apart: 29, of which 10 were waited for; matrix products, arithmetic and copies ran while one was open for 10% of the time, Pallas kernels for 46%

profile of v1, /device:TPU:0, one launch (start us, length us, event | category | flops | bytes accessed | tf_op | source)
XLA Modules:
  0.0 196.8 jit_solution(7053711646108772119)
XLA Ops:
  0.6 3.0 %collective-permute-start = (bf16[4,64,128]{2,1,0:T(8,128)(2,1)}, bf16[4,64,128]{2,1,0:T(8,128)(2,1)S(1)}, u32[]{:S(2)}, u32[]{:S(2)}) collective-permute-start(bf16[4,64,128]{2,1,0:T(8,128)(2,1)} %bitcast.79), channel_id=1, source_target_pairs={{0,8},{8,0},{16,24},{24,16},{1,9},{9,1},{17,25},{25,17},{2,10},{10... | collective-permute-start | bytes 196616 | tf_op jit(solution)/shard_map/ppermute | solution.py:489
  3.6 1.5 collective-permute-start.1
  5.2 3.1 %copy.33 = bf16[1,128,4,2,8,128]{5,1,4,0,3,2:T(8,128)(2,1)S(1)} copy(bf16[1,128,4,2,8,128]{5,4,3,2,1,0:T(8,128)(2,1)} %bitcast.64) | data formatting | bytes 4194304 | tf_op jit(solution)/shard_map/stack | solution.py:529
  8.3 1.4 copy.34
  10.0 1.6 fusion.4
  11.7 3.4 %dynamic-slice_bitcast_fusion = (bf16[2,8,128,128]{3,2,1,0:T(8,128)(2,1)S(1)}, bf16[2,8,128,128]{3,2,1,0:T(8,128)(2,1)}, bf16[2,8,128,128]{3,2,1,0:T(8,128)(2,1)...) fusion(bf16[4,1,2,8,128,128]{5,4,3,2,1,0:T(8,128)(2,1)S(1)} %ge, ...), kind=kLoop, calls=%fused_computation.5 | loop fusion | bytes 8388624 | tf_op jit(solution)/shard_map/jit(dynamic_index_in_dim)/squeeze | solution.py:534
  15.1 2.1 %collective-permute-start.3 = (bf16[4,4,64,128]{3,2,1,0:T(8,128)(2,1)S(1)}, bf16[4,4,64,128]{3,2,1,0:T(8,128)(2,1)S(1)}, u32[]{:S(2)}, u32[]{:S(2)}) collective-permute-start(bf16[4,4,64,128]{3,2,1,0:T(8,128)(2,1)S(1)} %pad_maximum_fusion.2), channel_id=1, source_target_pairs={{0,2},{1,3},{2,0},{3,1},{4,6},{5,7},{6,4},{7,5},{8,10},{9,11},{10,... | collective-permute-start | bytes 786440 | tf_op jit(solution)/shard_map/ppermute | solution.py:489
  17.2 1.5 collective-permute-start.6
  18.7 1.5 collective-permute-start.7
  20.7 2.6 %collective-permute-start.4 = (bf16[4,4,64,128]{3,2,1,0:T(8,128)(2,1)S(1)}, bf16[4,4,64,128]{3,2,1,0:T(8,128)(2,1)S(1)}, u32[]{:S(2)}, u32[]{:S(2)}) collective-permute-start(bf16[4,4,64,128]{3,2,1,0:T(8,128)(2,1)S(1)} %pad_maximum_fusion.2), channel_id=1, source_target_pairs={{0,4},{1,5},{2,6},{3,7},{4,0},{5,1},{6,2},{7,3},{8,12},{9,13},{10,... | collective-permute-start | bytes 786440 | tf_op jit(solution)/shard_map/ppermute | solution.py:489
  23.3 0.7 collective-permute-done.3
  24.0 4.1 %collective-permute-start.5 = (bf16[4,4,64,128]{3,2,1,0:T(8,128)(2,1)S(1)}, bf16[4,4,64,128]{3,2,1,0:T(8,128)(2,1)S(1)}, u32[]{:S(2)}, u32[]{:S(2)}) collective-permute-start(bf16[4,4,64,128]{3,2,1,0:T(8,128)(2,1)S(1)} %pad_maximum_fusion.2), channel_id=1, source_target_pairs={{0,6},{1,7},{2,4},{3,5},{4,2},{5,3},{6,0},{7,1},{8,14},{9,15},{10,... | collective-permute-start | bytes 786440 | tf_op jit(solution)/shard_map/ppermute | solution.py:489
  28.7 12.2 %collective-permute-done.4 = bf16[4,4,64,128]{3,2,1,0:T(8,128)(2,1)S(1)} collective-permute-done((bf16[4,4,64,128]{3,2,1,0:T(8,128)(2,1)S(1)}, bf16[4,4,64,128]{3,2,1,0:T(8,128)(2,1)S(1)}, u32[]{:S(2)}, u32[]{:S(2)}) %collective-permute-start.4) | collective-permute-done | bytes 262176 | tf_op jit(solution)/shard_map/ppermute | solution.py:489
  41.1 1.5 collective-permute-done.7.refs_2_
  43.2 0.8 copy.40.refs_5_
  47.0 1.5 collective-permute-start.10
  48.6 1.2 collective-permute-start.11
  49.7 0.8 collective-permute-start.9
  50.5 1.5 pad_maximum_fusion
  52.0 5.7 %shard_map.153.refs_4_ = f32[4,4,4,128,128]{4,3,2,1,0:T(8,128)} custom-call(s32[4,3]{1,0:T(4,128)} %tables_ref.5, s32[4]{0:T(128)} %lens_ref.5, s32[8]{0:T(128)} %multiply_add_fusion.col_pos_ref, s32[4]{0:T(128)} %iota_xor_fusion.row_pos_ref, bf16[8,4,4,64,128]{4,3,2,1,0:T(8,128)(2,1)} %bitcast.61, bf16[8,4,4,64,128]{4,3,2,1,0:T(8,128)(2,1)} %bitcast.62), custom_call_target="tpu_custom_call" | custom-call | tf_op jit(solution)/shard_map/pallas_call | solution.py:59
  57.8 40.8 %shard_map.154 = (bf16[8,128,128]{2,1,0:T(8,128)(2,1)}, bf16[8,128,128]{2,1,0:T(8,128)(2,1)}, bf16[8,128,128]{2,1,0:T(8,128)(2,1)}, bf16[8,128,128]{2,1,0:T(8,12...) custom-call(s32[4,3]{1,0:T(4,128)} %tables_ref.5, ...), custom_call_target="tpu_custom_call" | custom-call | flops 44040192000 | bytes 13631488 | tf_op jit(solution)/shard_map/pallas_call | solution.py:336
  98.6 1.3 collective-permute-start.13
  99.9 0.8 collective-permute-start.14
  100.7 1.4 collective-permute-start.15
  102.2 0.8 copy-done.14
  103.2 42.8 %shard_map.155 = (bf16[8,128,128]{2,1,0:T(8,128)(2,1)}, bf16[8,128,128]{2,1,0:T(8,128)(2,1)}, bf16[8,128,128]{2,1,0:T(8,128)(2,1)}, bf16[8,128,128]{2,1,0:T(8,12...) custom-call(s32[4,3]{1,0:T(4,128)} %tables_ref.5, s32[4]{0:T(128)} %lens_ref.5, ...), custom_call_target="tpu_custom_call" | custom-call | flops 44040192000 | bytes 13631488 | tf_op jit(solution)/shard_map/pallas_call | solution.py:336
  146.7 0.7 fusion.2.chosen_ref
  148.8 0.8 shard_map.156
  150.2 4.2 %collective-permute-start.20 = (bf16[928,128]{1,0:T(8,128)(2,1)S(1)}, bf16[928,128]{1,0:T(8,128)(2,1)S(1)}, u32[]{:S(2)}, u32[]{:S(2)}) collective-permute-start(bf16[928,128]{1,0:T(8,128)(2,1)S(1)} %get-tuple-element.113), channel_id=1, source_target_pairs={{0,2},{1,3},{2,0},{3,1},{4,6},{5,7},{6,4},{7,5},{8,10},{9,11},{10,... | collective-permute-start | bytes 712712 | tf_op jit(solution)/shard_map/ppermute | solution.py:489
  154.4 1.1 collective-permute-start.21
  155.5 1.4 collective-permute-start.22
  156.9 1.5 collective-permute-start.18
  158.7 6.3 %collective-permute-done.20.refs_0_ = bf16[928,128]{1,0:T(8,128)(2,1)S(1)} collective-permute-done((bf16[928,128]{1,0:T(8,128)(2,1)S(1)}, bf16[928,128]{1,0:T(8,128)(2,1)S(1)}, u32[]{:S(2)}, u32[]{:S(2)}) %collective-permute-start.20) | collective-permute-done | bytes 237600 | tf_op jit(solution)/shard_map/ppermute | solution.py:489
  165.0 1.5 collective-permute-start.19
  166.5 7.6 %collective-permute-done.21.refs_1_ = bf16[928,128]{1,0:T(8,128)(2,1)S(1)} collective-permute-done((bf16[928,128]{1,0:T(8,128)(2,1)S(1)}, bf16[928,128]{1,0:T(8,128)(2,1)S(1)}, u32[]{:S(2)}, u32[]{:S(2)}) %collective-permute-start.21) | collective-permute-done | bytes 237600 | tf_op jit(solution)/shard_map/ppermute | solution.py:489
  174.1 1.4 shard_map.157
  176.1 1.5 collective-permute-start.24
  177.7 1.4 collective-permute-start.25
  179.6 0.7 collective-permute-done.23.refs_0_
  180.3 0.7 collective-permute-done.24.refs_1_
  181.0 2.2 %collective-permute-done.25.refs_2_ = bf16[416,128]{1,0:T(8,128)(2,1)S(1)} collective-permute-done((bf16[416,128]{1,0:T(8,128)(2,1)S(1)}, bf16[416,128]{1,0:T(8,128)(2,1)S(1)}, u32[]{:S(2)}, u32[]{:S(2)}) %collective-permute-start.25) | collective-permute-done | bytes 106528 | tf_op jit(solution)/shard_map/ppermute | solution.py:489
  183.3 0.7 shard_map.158
  183.9 4.6 %collective-permute-start.26 = (bf16[160,128]{1,0:T(8,128)(2,1)S(1)}, bf16[160,128]{1,0:T(8,128)(2,1)S(1)}, u32[]{:S(2)}, u32[]{:S(2)}) collective-permute-start(bf16[160,128]{1,0:T(8,128)(2,1)S(1)} %get-tuple-element.121.refs_0_), channel_id=1, source_target_pairs={{0,2},{1,3},{2,0},{3,1},{4,6},{5,7},{6,4},{7,5},{8,10},{9,11},{10,... | collective-permute-start | bytes 122888 | tf_op jit(solution)/shard_map/ppermute | solution.py:489
  188.5 1.1 collective-permute-start.27
  189.6 1.5 collective-permute-start.28
  191.3 2.6 %collective-permute-done.27.refs_2_ = bf16[160,128]{1,0:T(8,128)(2,1)S(1)} collective-permute-done((bf16[160,128]{1,0:T(8,128)(2,1)S(1)}, bf16[160,128]{1,0:T(8,128)(2,1)S(1)}, u32[]{:S(2)}, u32[]{:S(2)}) %collective-permute-start.27) | collective-permute-done | bytes 40992 | tf_op jit(solution)/shard_map/ppermute | solution.py:489
  193.9 1.6 collective-permute-done.28.refs_3_
  195.5 1.3 shard_map.159
  (91 shorter events, 9.5 us)
Async XLA Ops:
  0.6 14.4 %collective-permute-start = (bf16[4,64,128]{2,1,0:T(8,128)(2,1)}, bf16[4,64,128]{2,1,0:T(8,128)(2,1)S(1)}, u32[]{:S(2)}, u32[]{:S(2)}) collective-permute-start(bf16[4,64,128]{2,1,0:T(8,128)(2,1)} %bitcast.79), channel_id=1, source_target_pairs={{0,8},{8,0},{16,24},{24,16},{1,9},{9,1},{17,25},{25,17},{2,10},{10... | collective-permute-start | bytes 196616 | tf_op jit(solution)/shard_map/ppermute | solution.py:489
  3.6 11.4 %collective-permute-start.1 = (bf16[4,64,128]{2,1,0:T(8,128)(2,1)}, bf16[4,64,128]{2,1,0:T(8,128)(2,1)S(1)}, u32[]{:S(2)}, u32[]{:S(2)}) collective-permute-start(bf16[4,64,128]{2,1,0:T(8,128)(2,1)} %bitcast.80), channel_id=1, source_target_pairs={{0,16},{8,24},{16,0},{24,8},{1,17},{9,25},{17,1},{25,9},{2,18},{10... | collective-permute-start | bytes 196616 | tf_op jit(solution)/shard_map/ppermute | solution.py:489
  5.2 9.9 %collective-permute-start.2 = (bf16[4,64,128]{2,1,0:T(8,128)(2,1)}, bf16[4,64,128]{2,1,0:T(8,128)(2,1)S(1)}, u32[]{:S(2)}, u32[]{:S(2)}) collective-permute-start(bf16[4,64,128]{2,1,0:T(8,128)(2,1)} %bitcast.81), channel_id=1, source_target_pairs={{0,24},{8,16},{16,8},{24,0},{1,25},{9,17},{17,9},{25,1},{2,26},{10... | collective-permute-start | bytes 196616 | tf_op jit(solution)/shard_map/ppermute | solution.py:489
  5.2 3.1 %copy-start.4 = (bf16[128,64,128]{2,1,0:T(8,128)(2,1)S(1)}, bf16[128,64,128]{2,1,0:T(8,128)(2,1)}, u32[]{:S(2)}) copy-start(bf16[128,64,128]{2,1,0:T(8,128)(2,1)} %param.11) | copy-start | bytes 6291460
  11.7 3.4 %copy-start.7 = (bf16[4,128,64]{1,2,0:T(8,128)(2,1)S(1)}, bf16[4,128,64]{1,2,0:T(8,128)(2,1)}, u32[]{:S(2)}) copy-start(bf16[4,128,64]{1,2,0:T(8,128)(2,1)} %param.12) | copy-start | bytes 196612
  11.7 16.5 %copy-start.8 = (bf16[128,128]{1,0:T(8,128)(2,1)S(1)}, bf16[128,128]{1,0:T(8,128)(2,1)}, u32[]{:S(2)}) copy-start(bf16[128,128]{1,0:T(8,128)(2,1)} %param.13) | copy-start | bytes 98308
  11.7 16.6 %copy-start.9 = (bf16[128,128]{1,0:T(8,128)(2,1)S(1)}, bf16[128,128]{1,0:T(8,128)(2,1)}, u32[]{:S(2)}) copy-start(bf16[128,128]{1,0:T(8,128)(2,1)} %param.14) | copy-start | bytes 98308
  11.7 16.7 %copy-start.10 = (bf16[128,128]{1,0:T(8,128)(2,1)S(1)}, bf16[128,128]{1,0:T(8,128)(2,1)}, u32[]{:S(2)}) copy-start(bf16[128,128]{1,0:T(8,128)(2,1)} %param.15) | copy-start | bytes 98308
  11.7 16.9 %copy-start.11 = (bf16[128,128]{1,0:T(8,128)(2,1)S(1)}, bf16[128,128]{1,0:T(8,128)(2,1)}, u32[]{:S(2)}) copy-start(bf16[128,128]{1,0:T(8,128)(2,1)} %param.16) | copy-start | bytes 98308
  15.1 8.9 %collective-permute-start.3 = (bf16[4,4,64,128]{3,2,1,0:T(8,128)(2,1)S(1)}, bf16[4,4,64,128]{3,2,1,0:T(8,128)(2,1)S(1)}, u32[]{:S(2)}, u32[]{:S(2)}) collective-permute-start(bf16[4,4,64,128]{3,2,1,0:T(8,128)(2,1)S(1)} %pad_maximum_fusion.2), channel_id=1, source_target_pairs={{0,2},{1,3},{2,0},{3,1},{4,6},{5,7},{6,4},{7,5},{8,10},{9,11},{10,... | collective-permute-start | bytes 786440 | tf_op jit(solution)/shard_map/ppermute | solution.py:489
  17.2 23.8 %collective-permute-start.6 = (bf16[2,8,128,128]{3,2,1,0:T(8,128)(2,1)}, bf16[2,8,128,128]{3,2,1,0:T(8,128)(2,1)}, u32[]{:S(2)}, u32[]{:S(2)}) collective-permute-start(bf16[2,8,128,128]{3,2,1,0:T(8,128)(2,1)} %get-tuple-element.69), channel_id=1, source_target_pairs={{0,8},{8,0},{16,24},{24,16},{1,9},{9,1},{17,25},{25,17},{2,10},{10... | collective-permute-start | bytes 1572872 | tf_op jit(solution)/shard_map/ppermute | solution.py:489
  18.7 23.8 %collective-permute-start.7 = (bf16[2,8,128,128]{3,2,1,0:T(8,128)(2,1)}, bf16[2,8,128,128]{3,2,1,0:T(8,128)(2,1)}, u32[]{:S(2)}, u32[]{:S(2)}) collective-permute-start(bf16[2,8,128,128]{3,2,1,0:T(8,128)(2,1)} %get-tuple-element.70), channel_id=1, source_target_pairs={{0,16},{8,24},{16,0},{24,8},{1,17},{9,25},{17,1},{25,9},{2,18},{10... | collective-permute-start | bytes 1572872 | tf_op jit(solution)/shard_map/ppermute | solution.py:489
  20.2 22.3 %collective-permute-start.8 = (bf16[2,8,128,128]{3,2,1,0:T(8,128)(2,1)}, bf16[2,8,128,128]{3,2,1,0:T(8,128)(2,1)}, u32[]{:S(2)}, u32[]{:S(2)}) collective-permute-start(bf16[2,8,128,128]{3,2,1,0:T(8,128)(2,1)} %get-tuple-element.71), channel_id=1, source_target_pairs={{0,24},{8,16},{16,8},{24,0},{1,25},{9,17},{17,9},{25,1},{2,26},{10... | collective-permute-start | bytes 1572872 | tf_op jit(solution)/shard_map/ppermute | solution.py:489
  20.7 20.2 %collective-permute-start.4 = (bf16[4,4,64,128]{3,2,1,0:T(8,128)(2,1)S(1)}, bf16[4,4,64,128]{3,2,1,0:T(8,128)(2,1)S(1)}, u32[]{:S(2)}, u32[]{:S(2)}) collective-permute-start(bf16[4,4,64,128]{3,2,1,0:T(8,128)(2,1)S(1)} %pad_maximum_fusion.2), channel_id=1, source_target_pairs={{0,4},{1,5},{2,6},{3,7},{4,0},{5,1},{6,2},{7,3},{8,12},{9,13},{10,... | collective-permute-start | bytes 786440 | tf_op jit(solution)/shard_map/ppermute | solution.py:489
  24.0 16.9 %collective-permute-start.5 = (bf16[4,4,64,128]{3,2,1,0:T(8,128)(2,1)S(1)}, bf16[4,4,64,128]{3,2,1,0:T(8,128)(2,1)S(1)}, u32[]{:S(2)}, u32[]{:S(2)}) collective-permute-start(bf16[4,4,64,128]{3,2,1,0:T(8,128)(2,1)S(1)} %pad_maximum_fusion.2), channel_id=1, source_target_pairs={{0,6},{1,7},{2,4},{3,5},{4,2},{5,3},{6,0},{7,1},{8,14},{9,15},{10,... | collective-permute-start | bytes 786440 | tf_op jit(solution)/shard_map/ppermute | solution.py:489
  42.5 8.0 %collective-permute-start.12 = (bf16[4,4,4,64,128]{4,3,2,1,0:T(8,128)(2,1)S(1)}, bf16[4,4,4,64,128]{4,3,2,1,0:T(8,128)(2,1)S(1)}, u32[]{:S(2)}, u32[]{:S(2)}) collective-permute-start(bf16[4,4,4,64,128]{4,3,2,1,0:T(8,128)(2,1)S(1)} %pad_maximum_fusion.1), channel_id=1, source_target_pairs={{0,1},{1,0},{2,3},{3,2},{4,5},{5,4},{6,7},{7,6},{8,9},{9,8},{10,11... | collective-permute-start | bytes 3145736 | tf_op jit(solution)/shard_map/ppermute | solution.py:489
  47.0 53.7 %collective-permute-start.10 = (bf16[2,8,128,128]{3,2,1,0:T(8,128)(2,1)}, bf16[2,8,128,128]{3,2,1,0:T(8,128)(2,1)S(1)}, u32[]{:S(2)}, u32[]{:S(2)}) collective-permute-start(bf16[2,8,128,128]{3,2,1,0:T(8,128)(2,1)} %get-tuple-element.78), channel_id=1, source_target_pairs={{0,16},{8,24},{16,0},{24,8},{1,17},{9,25},{17,1},{25,9},{2,18},{10... | collective-permute-start | bytes 1572872 | tf_op jit(solution)/shard_map/ppermute | solution.py:489
  48.6 53.6 %collective-permute-start.11 = (bf16[2,8,128,128]{3,2,1,0:T(8,128)(2,1)S(1)}, bf16[2,8,128,128]{3,2,1,0:T(8,128)(2,1)S(1)}, u32[]{:S(2)}, u32[]{:S(2)}) collective-permute-start(bf16[2,8,128,128]{3,2,1,0:T(8,128)(2,1)S(1)} %get-tuple-element.79), channel_id=1, source_target_pairs={{0,24},{8,16},{16,8},{24,0},{1,25},{9,17},{17,9},{25,1},{2,26},{10... | collective-permute-start | bytes 1572872 | tf_op jit(solution)/shard_map/ppermute | solution.py:489
  49.7 52.4 %collective-permute-start.9 = (bf16[2,8,128,128]{3,2,1,0:T(8,128)(2,1)S(1)}, bf16[2,8,128,128]{3,2,1,0:T(8,128)(2,1)S(1)}, u32[]{:S(2)}, u32[]{:S(2)}) collective-permute-start(bf16[2,8,128,128]{3,2,1,0:T(8,128)(2,1)S(1)} %get-tuple-element.77), channel_id=1, source_target_pairs={{0,8},{8,0},{16,24},{24,16},{1,9},{9,1},{17,25},{25,17},{2,10},{10... | collective-permute-start | bytes 1572872 | tf_op jit(solution)/shard_map/ppermute | solution.py:489
  98.6 47.4 %collective-permute-start.13 = (bf16[8,128,128]{2,1,0:T(8,128)(2,1)}, bf16[8,128,128]{2,1,0:T(8,128)(2,1)S(1)}, u32[]{:S(2)}, u32[]{:S(2)}) collective-permute-start(bf16[8,128,128]{2,1,0:T(8,128)(2,1)} %get-tuple-element.91), channel_id=1, source_target_pairs={{8,0},{0,8},{24,16},{16,24},{9,1},{1,9},{25,17},{17,25},{10,2},{2,... | collective-permute-start | bytes 786440 | tf_op jit(solution)/shard_map/ppermute | solution.py:489
  99.9 46.1 %collective-permute-start.14 = (bf16[8,128,128]{2,1,0:T(8,128)(2,1)}, bf16[8,128,128]{2,1,0:T(8,128)(2,1)S(1)}, u32[]{:S(2)}, u32[]{:S(2)}) collective-permute-start(bf16[8,128,128]{2,1,0:T(8,128)(2,1)} %get-tuple-element.92), channel_id=1, source_target_pairs={{16,0},{24,8},{0,16},{8,24},{17,1},{25,9},{1,17},{9,25},{18,2},{26... | collective-permute-start | bytes 786440 | tf_op jit(solution)/shard_map/ppermute | solution.py:489
  100.7 1.5 copy-start.13
  100.7 45.3 %collective-permute-start.15 = (bf16[8,128,128]{2,1,0:T(8,128)(2,1)}, bf16[8,128,128]{2,1,0:T(8,128)(2,1)S(1)}, u32[]{:S(2)}, u32[]{:S(2)}) collective-permute-start(bf16[8,128,128]{2,1,0:T(8,128)(2,1)} %get-tuple-element.93), channel_id=1, source_target_pairs={{24,0},{16,8},{8,16},{0,24},{25,1},{17,9},{9,17},{1,25},{26,2},{18... | collective-permute-start | bytes 786440 | tf_op jit(solution)/shard_map/ppermute | solution.py:489
  102.2 0.8 copy-start.14
  102.2 1.0 copy-start.15
  103.2 43.0 %copy-start.12 = (s32[4]{0:T(128)S(1)}, s32[4]{0:T(128)}, u32[]{:S(2)}) copy-start(s32[4]{0:T(128)} %lens_ref.5) | copy-start | bytes 52
  145.9 2.1 %copy-start.6 = (bf16[8,128,128]{2,1,0:T(8,128)(2,1)S(1)}, bf16[8,128,128]{2,1,0:T(8,128)(2,1)}, u32[]{:S(2)}) copy-start(bf16[8,128,128]{2,1,0:T(8,128)(2,1)} %get-tuple-element.94) | copy-start | bytes 786436
  145.9 2.9 %copy-start = (bf16[4,768,128]{2,1,0:T(8,128)(2,1)S(1)}, bf16[4,768,128]{2,1,0:T(8,128)(2,1)}, u32[]{:S(2)}) copy-start(bf16[4,768,128]{2,1,0:T(8,128)(2,1)} %get-tuple-element.98.keep_ref) | copy-start | bytes 2359300
  145.9 2.9 %copy-start.1 = (f32[640,128]{1,0:T(8,128)S(1)}, f32[640,128]{1,0:T(8,128)}, u32[]{:S(2)}) copy-start(f32[640,128]{1,0:T(8,128)} %get-tuple-element.100.weights_ref) | copy-start | bytes 983044
  146.0 2.8 %collective-permute-start.16 = (bf16[3712,128]{1,0:T(8,128)(2,1)}, bf16[3712,128]{1,0:T(8,128)(2,1)S(1)}, u32[]{:S(2)}, u32[]{:S(2)}) collective-permute-start(bf16[3712,128]{1,0:T(8,128)(2,1)} %get-tuple-element.99), channel_id=1, source_target_pairs={{0,1},{1,0},{2,3},{3,2},{4,5},{5,4},{6,7},{7,6},{8,9},{9,8},{10,11... | collective-permute-start | bytes 2850824 | tf_op jit(solution)/shard_map/ppermute | solution.py:489
  148.0 1.7 copy-start.18
  148.0 8.9 %copy-start.17 = (bf16[8,128,128]{2,1,0:T(8,128)(2,1)S(1)}, bf16[8,128,128]{2,1,0:T(8,128)(2,1)}, u32[]{:S(2)}) copy-start(bf16[8,128,128]{2,1,0:T(8,128)(2,1)} %get-tuple-element.110) | copy-start | bytes 786436
  148.0 10.4 %copy-start.5 = (bf16[8,128,128]{2,1,0:T(8,128)(2,1)S(1)}, bf16[8,128,128]{2,1,0:T(8,128)(2,1)}, u32[]{:S(2)}) copy-start(bf16[8,128,128]{2,1,0:T(8,128)(2,1)} %get-tuple-element.108) | copy-start | bytes 786436
  148.3 16.7 %copy-start.16 = (bf16[8,128,128]{2,1,0:T(8,128)(2,1)S(1)}, bf16[8,128,128]{2,1,0:T(8,128)(2,1)}, u32[]{:S(2)}) copy-start(bf16[8,128,128]{2,1,0:T(8,128)(2,1)} %get-tuple-element.111) | copy-start | bytes 786436
  148.3 25.8 %copy-start.2 = (s32[4]{0:T(128)S(1)}, s32[4]{0:T(128)}, u32[]{:S(2)}) copy-start(s32[4]{0:T(128)} %pad_add_fusion.owners_ref) | copy-start | bytes 52
  149.7 28.0 %collective-permute-start.17 = (bf16[8,128,128]{2,1,0:T(8,128)(2,1)S(1)}, bf16[8,128,128]{2,1,0:T(8,128)(2,1)S(1)}, u32[]{:S(2)}, u32[]{:S(2)}) collective-permute-start(bf16[8,128,128]{2,1,0:T(8,128)(2,1)S(1)} %copy-done.18), channel_id=1, source_target_pairs={{8,0},{0,8},{24,16},{16,24},{9,1},{1,9},{25,17},{17,25},{10,2},{2,... | collective-permute-start | bytes 786440 | tf_op jit(solution)/shard_map/ppermute | solution.py:489
  150.2 14.8 %collective-permute-start.20 = (bf16[928,128]{1,0:T(8,128)(2,1)S(1)}, bf16[928,128]{1,0:T(8,128)(2,1)S(1)}, u32[]{:S(2)}, u32[]{:S(2)}) collective-permute-start(bf16[928,128]{1,0:T(8,128)(2,1)S(1)} %get-tuple-element.113), channel_id=1, source_target_pairs={{0,2},{1,3},{2,0},{3,1},{4,6},{5,7},{6,4},{7,5},{8,10},{9,11},{10,... | collective-permute-start | bytes 712712 | tf_op jit(solution)/shard_map/ppermute | solution.py:489
  154.4 19.7 %collective-permute-start.21 = (bf16[928,128]{1,0:T(8,128)(2,1)S(1)}, bf16[928,128]{1,0:T(8,128)(2,1)S(1)}, u32[]{:S(2)}, u32[]{:S(2)}) collective-permute-start(bf16[928,128]{1,0:T(8,128)(2,1)S(1)} %get-tuple-element.114), channel_id=1, source_target_pairs={{0,4},{1,5},{2,6},{3,7},{4,0},{5,1},{6,2},{7,3},{8,12},{9,13},{10,... | collective-permute-start | bytes 712712 | tf_op jit(solution)/shard_map/ppermute | solution.py:489
  155.5 18.6 %collective-permute-start.22 = (bf16[928,128]{1,0:T(8,128)(2,1)S(1)}, bf16[928,128]{1,0:T(8,128)(2,1)S(1)}, u32[]{:S(2)}, u32[]{:S(2)}) collective-permute-start(bf16[928,128]{1,0:T(8,128)(2,1)S(1)} %get-tuple-element.115), channel_id=1, source_target_pairs={{0,6},{1,7},{2,4},{3,5},{4,2},{5,3},{6,0},{7,1},{8,14},{9,15},{10,... | collective-permute-start | bytes 712712 | tf_op jit(solution)/shard_map/ppermute | solution.py:489
  156.9 22.4 %collective-permute-start.18 = (bf16[8,128,128]{2,1,0:T(8,128)(2,1)S(1)}, bf16[8,128,128]{2,1,0:T(8,128)(2,1)S(1)}, u32[]{:S(2)}, u32[]{:S(2)}) collective-permute-start(bf16[8,128,128]{2,1,0:T(8,128)(2,1)S(1)} %copy-done.17), channel_id=1, source_target_pairs={{16,0},{24,8},{0,16},{8,24},{17,1},{25,9},{1,17},{9,25},{18,2},{26... | collective-permute-start | bytes 786440 | tf_op jit(solution)/shard_map/ppermute | solution.py:489
  165.0 26.1 %collective-permute-start.19 = (bf16[8,128,128]{2,1,0:T(8,128)(2,1)S(1)}, bf16[8,128,128]{2,1,0:T(8,128)(2,1)S(1)}, u32[]{:S(2)}, u32[]{:S(2)}) collective-permute-start(bf16[8,128,128]{2,1,0:T(8,128)(2,1)S(1)} %copy-done.16), channel_id=1, source_target_pairs={{24,0},{16,8},{8,16},{0,24},{25,1},{17,9},{9,17},{1,25},{26,2},{18... | collective-permute-start | bytes 786440 | tf_op jit(solution)/shard_map/ppermute | solution.py:489
  175.5 4.8 %collective-permute-start.23 = (bf16[416,128]{1,0:T(8,128)(2,1)S(1)}, bf16[416,128]{1,0:T(8,128)(2,1)S(1)}, u32[]{:S(2)}, u32[]{:S(2)}) collective-permute-start(bf16[416,128]{1,0:T(8,128)(2,1)S(1)} %get-tuple-element.117), channel_id=1, source_target_pairs={{0,8},{8,0},{16,24},{24,16},{1,9},{9,1},{17,25},{25,17},{2,10},{10... | collective-permute-start | bytes 319496 | tf_op jit(solution)/shard_map/ppermute | solution.py:489
  176.1 4.9 %collective-permute-start.24 = (bf16[416,128]{1,0:T(8,128)(2,1)S(1)}, bf16[416,128]{1,0:T(8,128)(2,1)S(1)}, u32[]{:S(2)}, u32[]{:S(2)}) collective-permute-start(bf16[416,128]{1,0:T(8,128)(2,1)S(1)} %get-tuple-element.118), channel_id=1, source_target_pairs={{0,16},{8,24},{16,0},{24,8},{1,17},{9,25},{17,1},{25,9},{2,18},{10... | collective-permute-start | bytes 319496 | tf_op jit(solution)/shard_map/ppermute | solution.py:489
  177.7 5.6 %collective-permute-start.25 = (bf16[416,128]{1,0:T(8,128)(2,1)S(1)}, bf16[416,128]{1,0:T(8,128)(2,1)S(1)}, u32[]{:S(2)}, u32[]{:S(2)}) collective-permute-start(bf16[416,128]{1,0:T(8,128)(2,1)S(1)} %get-tuple-element.119), channel_id=1, source_target_pairs={{0,24},{8,16},{16,8},{24,0},{1,25},{9,17},{17,9},{25,1},{2,26},{10... | collective-permute-start | bytes 319496 | tf_op jit(solution)/shard_map/ppermute | solution.py:489
  183.9 7.4 %collective-permute-start.26 = (bf16[160,128]{1,0:T(8,128)(2,1)S(1)}, bf16[160,128]{1,0:T(8,128)(2,1)S(1)}, u32[]{:S(2)}, u32[]{:S(2)}) collective-permute-start(bf16[160,128]{1,0:T(8,128)(2,1)S(1)} %get-tuple-element.121.refs_0_), channel_id=1, source_target_pairs={{0,2},{1,3},{2,0},{3,1},{4,6},{5,7},{6,4},{7,5},{8,10},{9,11},{10,... | collective-permute-start | bytes 122888 | tf_op jit(solution)/shard_map/ppermute | solution.py:489
  188.5 5.3 %collective-permute-start.27 = (bf16[160,128]{1,0:T(8,128)(2,1)S(1)}, bf16[160,128]{1,0:T(8,128)(2,1)S(1)}, u32[]{:S(2)}, u32[]{:S(2)}) collective-permute-start(bf16[160,128]{1,0:T(8,128)(2,1)S(1)} %get-tuple-element.121.refs_0_), channel_id=1, source_target_pairs={{0,4},{1,5},{2,6},{3,7},{4,0},{5,1},{6,2},{7,3},{8,12},{9,13},{10,... | collective-permute-start | bytes 122888 | tf_op jit(solution)/shard_map/ppermute | solution.py:489
  189.6 5.9 %collective-permute-start.28 = (bf16[160,128]{1,0:T(8,128)(2,1)S(1)}, bf16[160,128]{1,0:T(8,128)(2,1)S(1)}, u32[]{:S(2)}, u32[]{:S(2)}) collective-permute-start(bf16[160,128]{1,0:T(8,128)(2,1)S(1)} %get-tuple-element.121.refs_0_), channel_id=1, source_target_pairs={{0,6},{1,7},{2,4},{3,5},{4,2},{5,3},{6,0},{7,1},{8,14},{9,15},{10,... | collective-permute-start | bytes 122888 | tf_op jit(solution)/shard_map/ppermute | solution.py:489
  191.3 5.5 %copy-start.3 = (bf16[128,64,128]{2,1,0:T(8,128)(2,1)}, bf16[128,64,128]{2,1,0:T(8,128)(2,1)S(1)}, u32[]{:S(2)}) copy-start(bf16[128,64,128]{2,1,0:T(8,128)(2,1)S(1)} %copy_dynamic-update-slice_fusion) | copy-start | bytes 6291460
